TPU v7x, 32 devices: a whole 2x2x4 slice. The times are simulated.
32 devices in a mesh: dp: 8 (over z, x), tensor: 4 (over y, core).
Axes of the slice: x: 2, y: 2, z: 4, core: 2. Of those that a mesh axis runs over, the one named last changes fastest.
Arguments:
- block_input: float32 [2048, 768], P('dp'), may hold values from -6 to 6
- first_gain: float32 [768], replicated, may hold values from 0.5 to 1.5
- first_shift: float32 [768], replicated, may hold values from -3 to 3
- input_weight: bfloat16 [768, 2304], P(None, 'tensor'), may hold values from -1.5 to 1.5
- input_bias: float32 [1536], P('tensor'), may hold values from -3 to 3
- output_weight: bfloat16 [768, 768], P('tensor'), may hold values from -0.875 to 0.875
- output_bias: float32 [768], replicated, may hold values from -3 to 3
- second_gain: float32 [768], replicated, may hold values from 0.5 to 1.5
- second_shift: float32 [768], replicated, may hold values from -3 to 3
- expand_weight: bfloat16 [768, 3072], P(None, 'tensor'), may hold values from -0.21875 to 0.21875
- expand_bias: float32 [3072], P('tensor'), may hold values from -3 to 3
- reduce_weight: bfloat16 [3072, 768], P('tensor'), may hold values from -0.109375 to 0.109375
- reduce_bias: float32 [768], replicated, may hold values from -3 to 3
- output_grad: float32 [2048, 768], P('dp'), may hold values from -6 to 6
- segment_ids: int32 [2048], replicated, may hold values from 0 to 15, never falling along the last dimension, each value on 1 to 256 neighbouring positions
- shard_counts: int32 [8], replicated, may hold values from 128 to 256, as said below
Outputs:
- block_output: float32 [2048, 768], P(('dp', 'tensor'))
- input_grad: float32 [2048, 768], P(('dp', 'tensor'))
- first_gain_grad: float32 [768], P('dp')
- first_shift_grad: float32 [768], P('dp')
- input_weight_grad: float32 [768, 2304], P('dp', 'tensor')
- input_bias_grad: float32 [1536], P(('tensor', 'dp'))
- output_weight_grad: float32 [768, 768], P('tensor', 'dp')
- output_bias_grad: float32 [768], P('dp')
- second_gain_grad: float32 [768], P('dp')
- second_shift_grad: float32 [768], P('dp')
- expand_weight_grad: float32 [768, 3072], P('dp', 'tensor')
- expand_bias_grad: float32 [3072], P(('tensor', 'dp'))
- reduce_weight_grad: float32 [3072, 768], P('tensor', 'dp')
- reduce_bias_grad: float32 [768], P('dp')
Inputs may be any that keep to these rules, and one draw needn't show every extreme that they name: `segment_ids`: never falling along the token slots; one sequence covers at most 256 consecutive slots, dead slots included, and some sequence covers exactly 256. `shard_counts`: the live slots of a shard are its first ones; some shard is full in every draw.
All inputs are finite; a program needn't handle non-finite values.
Results may differ from a plain program's by a relative error of at most 0.0092.
Values may be sent and summed in bfloat16 or wider, within the bound.
A program may use at most 64 MiB of HBM per device.

v0:
```python
import jax
import jax.numpy as jnp
from jax import lax
from jax.sharding import PartitionSpec as P

HEAD_DIM = 64


EPSILON = 1e-05
GELU_COEF = 0.7978845608028654
CUBIC = 0.044715


def from_behind(value, axis, steps):
    count = lax.axis_size(axis)
    first, last = (max(0, -steps), min(count, count - steps))
    return lax.ppermute(value, axis, [(source, source + steps) for source in range(first, last)])


def layer_norm(values_in, gain_row, shift_row):
    centred = values_in - jnp.mean(values_in, axis=-1, keepdims=True)
    reciprocal = lax.rsqrt(jnp.mean(centred * centred, axis=-1, keepdims=True) + EPSILON)
    normed = centred * reciprocal
    return (normed * gain_row + shift_row, normed, reciprocal)


def norm_back(grad_in, normed, reciprocal, gain_row):
    scaled = grad_in * gain_row
    spread = (
        scaled
        - jnp.mean(scaled, axis=-1, keepdims=True)
        - normed * jnp.mean(scaled * normed, axis=-1, keepdims=True)
    )
    return (reciprocal * spread, jnp.sum(grad_in * normed, axis=0), jnp.sum(grad_in, axis=0))


def gelu_parts(pre_act):
    tanh_value = jnp.tanh(GELU_COEF * (pre_act + CUBIC * pre_act * pre_act * pre_act))
    result = 0.5 * pre_act * (1.0 + tanh_value)
    slope_value = 0.5 * (1.0 + tanh_value) + 0.5 * pre_act * (
        1.0 - tanh_value * tanh_value
    ) * GELU_COEF * (1.0 + 3.0 * CUBIC * pre_act * pre_act)
    return (result, slope_value)


def full_bias(pairs, group_heads):
    shaped = pairs.reshape(group_heads, 2, HEAD_DIM)
    return jnp.stack([shaped[:, 0], jnp.zeros_like(shaped[:, 0]), shaped[:, 1]], axis=1).reshape(
        group_heads * 3 * HEAD_DIM
    )


def masked_scores(queries, key_rows, allowed):
    scores = jnp.einsum(
        "qhd,khd->hqk", queries, key_rows, preferred_element_type=jnp.float32
    ) * HEAD_DIM ** (-0.5)
    return jnp.where(allowed[None], scores, -1e30)


def per_device(
    block_input,
    first_gain,
    first_shift,
    input_weight,
    input_bias,
    output_weight,
    output_bias,
    second_gain,
    second_shift,
    expand_weight,
    expand_bias,
    reduce_weight,
    reduce_bias,
    output_grad,
    segment_ids,
    shard_counts,
):
    f32 = jnp.float32
    b16 = jnp.bfloat16
    block_rows = block_input.shape[0]
    group_heads = output_weight.shape[0] // HEAD_DIM
    group_width = group_heads * HEAD_DIM
    score_scale = HEAD_DIM ** (-0.5)
    tensor_count = lax.axis_size("tensor")
    share_rows = block_rows // tensor_count
    row_start = lax.axis_index("tensor") * share_rows

    def own_rows(values):
        return lax.dynamic_slice_in_dim(values, row_start, share_rows, 0)

    shard_index = lax.axis_index("dp")
    prior_index = jnp.maximum(shard_index - 1, 0)
    position = jnp.arange(block_rows, dtype=jnp.int32)
    own_ids = lax.dynamic_slice_in_dim(segment_ids, shard_index * block_rows, block_rows)
    prior_ids = lax.dynamic_slice_in_dim(segment_ids, prior_index * block_rows, block_rows)
    own_live = position < shard_counts[shard_index]
    prior_live = (position < shard_counts[prior_index]) & (shard_index > 0)
    diagonal = position[None, :] == position[:, None]
    same_own = (
        (own_ids[:, None] == own_ids[None, :])
        & (position[None, :] <= position[:, None])
        & (own_live[None, :] | diagonal)
    )
    same_prior = (own_ids[:, None] == prior_ids[None, :]) & prior_live[None, :]
    allowed = jnp.concatenate([same_prior, same_own], axis=1)
    live_col = own_live.astype(f32)[:, None]
    first_out, normed1, recip1 = layer_norm(block_input, first_gain, first_shift)
    first_in = first_out.astype(b16)
    mixed = jnp.dot(first_in, input_weight, preferred_element_type=f32) + full_bias(
        input_bias, group_heads
    )
    mixed = mixed.astype(b16).reshape(block_rows, group_heads, 3, HEAD_DIM)
    queries = mixed[:, :, 0]
    own_pair = jnp.concatenate([mixed[:, :, 1], mixed[:, :, 2]], axis=1).reshape(
        block_rows, 2 * group_width
    )
    prior_pair = from_behind(own_pair, "dp", 1).reshape(block_rows, 2 * group_heads, HEAD_DIM)
    key_rows = jnp.concatenate([prior_pair[:, :group_heads], mixed[:, :, 1]], axis=0)
    value_rows = jnp.concatenate([prior_pair[:, group_heads:], mixed[:, :, 2]], axis=0)
    scores = masked_scores(queries, key_rows, allowed)
    row_top = jnp.max(scores, axis=-1, keepdims=True)
    logsum = row_top + jnp.log(jnp.sum(jnp.exp(scores - row_top), axis=-1, keepdims=True))
    soft16 = jnp.exp(scores - logsum).astype(b16)
    attended = (
        jnp.einsum("hqk,khd->qhd", soft16, value_rows, preferred_element_type=f32)
        .astype(b16)
        .reshape(block_rows, group_width)
    )
    hidden_rows = (
        own_rows(block_input)
        + lax.psum_scatter(
            jnp.dot(attended, output_weight, preferred_element_type=f32),
            "tensor",
            scatter_dimension=0,
            tiled=True,
        )
        + output_bias
    )
    second_out, normed2, recip2 = layer_norm(hidden_rows, second_gain, second_shift)
    second_in = lax.all_gather(second_out.astype(b16), "tensor", axis=0, tiled=True)
    pre_act = jnp.dot(second_in, expand_weight, preferred_element_type=f32) + expand_bias
    activ, gelu_slope = gelu_parts(pre_act)
    activated = activ.astype(b16)
    feed_rows = lax.psum_scatter(
        jnp.dot(activated, reduce_weight, preferred_element_type=f32),
        "tensor",
        scatter_dimension=0,
        tiled=True,
    )
    block_output = own_rows(live_col) * (hidden_rows + feed_rows + reduce_bias)
    grad_y = live_col * output_grad
    grad_y16 = grad_y.astype(b16)
    reduce_weight_grad = jnp.einsum("rk,rd->kd", activated, grad_y16, preferred_element_type=f32)
    reduce_bias_grad = jnp.sum(grad_y, axis=0)
    grad_pre = (
        jnp.einsum("rd,kd->rk", grad_y16, reduce_weight, preferred_element_type=f32) * gelu_slope
    )
    grad_pre16 = grad_pre.astype(b16)
    expand_weight_grad = jnp.einsum("rd,rk->dk", second_in, grad_pre16, preferred_element_type=f32)
    expand_bias_grad = jnp.sum(grad_pre, axis=0)
    grad_norm2 = lax.psum_scatter(
        jnp.einsum("rk,dk->rd", grad_pre16, expand_weight, preferred_element_type=f32),
        "tensor",
        scatter_dimension=0,
        tiled=True,
    )
    back2, gain_part, shift_part = norm_back(grad_norm2, normed2, recip2, second_gain)
    grad_rows = own_rows(grad_y) + back2
    gathered_hidden, part_sums = (
        lax.all_gather(grad_rows, "tensor", axis=0, tiled=True),
        lax.all_gather(jnp.stack([gain_part, shift_part], axis=0), "tensor", axis=0, tiled=True),
    )
    summed_parts = jnp.sum(part_sums.reshape(tensor_count, 2, part_sums.shape[1]), axis=0)
    second_gain_grad = summed_parts[0]
    second_shift_grad = summed_parts[1]
    grad_hidden16 = gathered_hidden.astype(b16)
    output_bias_grad = jnp.sum(gathered_hidden, axis=0)
    output_weight_grad = jnp.einsum(
        "rk,rd->kd", attended, grad_hidden16, preferred_element_type=f32
    )
    grad_att = (
        jnp.einsum("rd,kd->rk", grad_hidden16, output_weight, preferred_element_type=f32)
        .astype(b16)
        .reshape(block_rows, group_heads, HEAD_DIM)
    )
    scores = masked_scores(queries, key_rows, allowed)
    soft = jnp.exp(scores - logsum)
    grad_soft = jnp.einsum("qhd,khd->hqk", grad_att, value_rows, preferred_element_type=f32)
    delta = jnp.sum(soft * grad_soft, axis=-1, keepdims=True)
    grad_scores = (score_scale * soft * (grad_soft - delta)).astype(b16)
    grad_queries = jnp.einsum("hqk,khd->qhd", grad_scores, key_rows, preferred_element_type=f32)
    grad_keys = jnp.einsum("hqk,qhd->khd", grad_scores, queries, preferred_element_type=f32)
    grad_values = jnp.einsum("hqk,qhd->khd", soft.astype(b16), grad_att, preferred_element_type=f32)
    back_pair = jnp.concatenate([grad_keys[:block_rows], grad_values[:block_rows]], axis=1).reshape(
        block_rows, 2 * group_width
    )
    from_next = from_behind(back_pair, "dp", -1).reshape(block_rows, 2 * group_heads, HEAD_DIM)
    grad_mixed = jnp.stack(
        [
            grad_queries,
            grad_keys[block_rows:] + from_next[:, :group_heads],
            grad_values[block_rows:] + from_next[:, group_heads:],
        ],
        axis=2,
    )
    bias_sums = jnp.sum(grad_mixed, axis=0)
    input_bias_grad = jnp.stack([bias_sums[:, 0], bias_sums[:, 2]], axis=1).reshape(2 * group_width)
    grad_mixed16 = grad_mixed.reshape(block_rows, 3 * group_width).astype(b16)
    input_weight_grad = jnp.einsum("rd,rc->dc", first_in, grad_mixed16, preferred_element_type=f32)
    norm1_part = jnp.einsum("rc,dc->rd", grad_mixed16, input_weight, preferred_element_type=f32)
    grad_norm1 = lax.psum(norm1_part, "tensor")
    back1, first_gain_grad, first_shift_grad = norm_back(grad_norm1, normed1, recip1, first_gain)
    input_grad = grad_rows + own_rows(back1)
    every_grad = tuple(
        (
            lax.psum_scatter(first_gain_grad, "dp", scatter_dimension=0, tiled=True),
            lax.psum_scatter(first_shift_grad, "dp", scatter_dimension=0, tiled=True),
            lax.psum_scatter(input_weight_grad, "dp", scatter_dimension=0, tiled=True),
            lax.psum_scatter(input_bias_grad, "dp", scatter_dimension=0, tiled=True),
            lax.psum_scatter(output_weight_grad, "dp", scatter_dimension=1, tiled=True),
            lax.psum_scatter(output_bias_grad, "dp", scatter_dimension=0, tiled=True),
            lax.psum_scatter(second_gain_grad, "dp", scatter_dimension=0, tiled=True),
            lax.psum_scatter(second_shift_grad, "dp", scatter_dimension=0, tiled=True),
            lax.psum_scatter(expand_weight_grad, "dp", scatter_dimension=0, tiled=True),
            lax.psum_scatter(expand_bias_grad, "dp", scatter_dimension=0, tiled=True),
            lax.psum_scatter(reduce_weight_grad, "dp", scatter_dimension=1, tiled=True),
            lax.psum_scatter(reduce_bias_grad, "dp", scatter_dimension=0, tiled=True),
        )
    )
    return (
        block_output,
        input_grad,
        every_grad[0],
        every_grad[1],
        every_grad[2],
        every_grad[3],
        every_grad[4],
        every_grad[5],
        every_grad[6],
        every_grad[7],
        every_grad[8],
        every_grad[9],
        every_grad[10],
        every_grad[11],
    )


def solution(mesh):
    placed = (
        P("dp", None),
        P(),
        P(),
        P(None, "tensor"),
        P("tensor"),
        P("tensor", None),
        P(),
        P(),
        P(),
        P(None, "tensor"),
        P("tensor"),
        P("tensor", None),
        P(),
        P("dp", None),
        P(),
        P(),
    )
    return jax.shard_map(
        per_device,
        mesh=mesh,
        in_specs=placed,
        out_specs=(
            P(("dp", "tensor"), None),
            P(("dp", "tensor"), None),
            P("dp"),
            P("dp"),
            P("dp", "tensor"),
            P(("tensor", "dp")),
            P("tensor", "dp"),
            P("dp"),
            P("dp"),
            P("dp"),
            P("dp", "tensor"),
            P(("tensor", "dp")),
            P("tensor", "dp"),
            P("dp"),
        ),
        check_vma=False,
    )
```

profile of v0, /device:TPU:9, one launch (start us, length us, event | category | flops | bytes accessed | tf_op | source)
XLA Modules:
  0.0 465.0 jit_solution(1177759240771924943)
XLA Ops:
  7.3 1.4 reduce_sum.171
  11.1 1.6 fusion
  13.6 3.1 collective-permute-start
  19.7 2.5 collective-permute-done
  22.2 1.6 fusion.44
  28.0 2.7 fusion.37
  30.7 20.5 %reduce-scatter.10.cloned.1.call-done = f32[64,768]{1,0:T(8,128)} async-done(((f32[256,768]{1,0:T(8,128)}), f32[64,768]{1,0:T(8,128)}) %reduce-scatter.10.cloned.1.call-update) | async-done | bytes 196624 | tf_op jit(solution)/shard_map/reduce_scatter | solution.py:131
  53.5 6.7 %all_gather.9 = bf16[256,768]{1,0:T(8,128)(2,1)S(1)} all-gather(bf16[64,768]{1,0:T(8,128)(2,1)S(1)} %add_convert_fusion.1), channel_id=1, replica_groups=mesh['dp'=8,'tensor'=4] {'tensor'}, dimensions={0}, use_global_device_ids=true | all-gather | bytes 491520 | tf_op jit(solution)/shard_map/all_gather | solution.py:140
  63.6 1.4 fusion.23
  65.1 2.6 fusion.35
  69.0 19.2 %reduce-scatter.14.cloned.1.call-done = f32[64,768]{1,0:T(8,128)} async-done(((f32[256,768]{1,0:T(8,128)}), f32[64,768]{1,0:T(8,128)}) %reduce-scatter.14.cloned.1.call-update) | async-done | bytes 196624 | tf_op jit(solution)/shard_map/reduce_scatter | solution.py:161
  88.2 1.7 multiply_reduce_fusion.4
  91.0 23.1 %reduce-scatter.12.cloned.1.call-done = f32[64,768]{1,0:T(8,128)} async-done(((f32[256,768]{1,0:T(8,128)}), f32[64,768]{1,0:T(8,128)}) %reduce-scatter.12.cloned.1.call-update) | async-done | bytes 196624 | tf_op jit(solution)/shard_map/reduce_scatter | solution.py:144
  114.1 2.1 multiply_add_fusion.1
  116.2 8.7 %all_gather.10 = f32[256,768]{1,0:T(8,128)S(1)} all-gather(f32[64,768]{1,0:T(8,128)S(1)} %get-tuple-element.41), channel_id=1, replica_groups=mesh['dp'=8,'tensor'=4] {'tensor'}, dimensions={0}, use_global_device_ids=true | all-gather | bytes 983040 | tf_op jit(solution)/shard_map/all_gather | solution.py:170
  128.9 3.1 collective-permute-start.1
  132.3 9.0 %collective-permute-done.1 = f32[256,384]{0,1:T(8,128)S(1)} collective-permute-done((f32[256,384]{0,1:T(8,128)S(1)}, f32[256,384]{0,1:T(8,128)S(1)}, u32[]{:S(2)}, u32[]{:S(2)}) %collective-permute-start.1) | collective-permute-done | bytes 393248 | tf_op jit(solution)/shard_map/ppermute | solution.py:17
  143.0 1.4 fusion.47
  144.5 2.1 convolution_bitcast_fusion
  146.8 1.9 fusion.21
  149.8 3.2 fusion.25
  154.2 2.8 fusion.29
  161.6 6.1 %all-gather = f32[4,2,768]{2,1,0:T(2,128)S(1)} all-gather(f32[1,2,768]{2,1,0:T(2,128)S(1)} %maximum_bitcast_fusion), channel_id=1, replica_groups=mesh['dp'=8,'tensor'=4] {'tensor'}, dimensions={0}, use_global_device_ids=true | all-gather | bytes 30720 | tf_op jit(solution)/shard_map/all_gather | solution.py:171
  169.1 9.9 %all-reduce.11.cloned.1.call-done = f32[256,768]{1,0:T(8,128)} async-done(((f32[256,768]{1,0:T(8,128)}), f32[256,768]{1,0:T(8,128)}) %all-reduce.11.cloned.1.call-update) | async-done | bytes 786448 | tf_op jit(solution)/shard_map/psum | solution.py:211
  179.0 2.4 fusion.36
  181.4 27.8 %all-reduce.8 = (f32[768]{0:T(1024)S(1)}, f32[768]{0:T(1024)S(1)}, f32[384]{0:T(512)S(1)}, f32[768]{0:T(1024)S(1)}, f32[768]{0:T(1024)S(1)}, /*index=5*/f32[768]{0:T(1024)S(1)}, f32[768]{0:T(1024)S(1)}, f32[768]{0:T(1024)S(1)}) all-reduce(f32[768]{0:T(1024)S(1)} %get-tuple-element.15, ...), channel_id=5, replica_groups=mesh['dp'=8,'tensor'=4] {'dp'}, use_global_device_ids=true, to_apply=%region_16.17.clone | all-reduce | flops 5760 | bytes 46080
  214.1 1.7 fusion.16
  215.8 28.1 %reduce-scatter.22.cloned.1.call-done = f32[96,192]{1,0:T(8,128)} async-done(((f32[768,192]{1,0:T(8,128)}), f32[96,192]{1,0:T(8,128)}) %reduce-scatter.22.cloned.1.call-update) | async-done | bytes 73744
  243.9 1.6 copy.47
  245.5 70.4 %reduce-scatter.18.cloned.1.call-done = f32[96,768]{1,0:T(8,128)} async-done(((f32[768,768]{1,0:T(8,128)}), f32[96,768]{1,0:T(8,128)}) %reduce-scatter.18.cloned.1.call-update) | async-done | bytes 294928 | tf_op jit(solution)/shard_map/reduce_scatter | solution.py:224
  316.0 72.2 %reduce-scatter.20.cloned.1.call-done = f32[768,96]{0,1:T(8,128)} async-done(((f32[768,768]{0,1:T(8,128)}), f32[768,96]{0,1:T(8,128)}) %reduce-scatter.20.cloned.1.call-update) | async-done | bytes 294928 | tf_op jit(solution)/shard_map/reduce_scatter | solution.py:226
  388.1 70.0 %reduce-scatter.16.cloned.1.call-done = f32[96,576]{1,0:T(8,128)} async-done(((f32[768,576]{1,0:T(8,128)}), f32[96,576]{1,0:T(8,128)}) %reduce-scatter.16.cloned.1.call-update) | async-done | bytes 221200 | tf_op jit(solution)/shard_map/reduce_scatter | solution.py:218
  (187 shorter events, 36.1 us)
Async XLA Ops:
  7.2 54.3 %copy-start = (bf16[768,768]{1,0:T(8,128)(2,1)S(1)}, bf16[768,768]{1,0:T(8,128)(2,1)}, u32[]{:S(2)}) copy-start(bf16[768,768]{1,0:T(8,128)(2,1)} %param.27) | copy-start | bytes 3538948
  7.2 3.9 copy-start.36
  7.2 44.0 %reduce-scatter.10.cloned.1.call-start = ((), (), s32[]{:S(2)}) async-start(), calls=%async_computation.7 | async-start | bytes 983040 | tf_op jit(solution)/shard_map/reduce_scatter | solution.py:131
  10.8 8.8 %copy-start.6 = (f32[256,768]{1,0:T(8,128)}, f32[256,768]{1,0:T(8,128)S(1)}, u32[]{:S(2)}) copy-start(f32[256,768]{1,0:T(8,128)S(1)} %subtract_multiply_fusion) | copy-start | bytes 2359300
  10.8 5.9 %copy-start.47 = (s32[8]{0:T(128)S(1)}, s32[8]{0:T(128)}, u32[]{:S(2)}) copy-start(s32[8]{0:T(128)} %param.31) | copy-start | bytes 100
  13.6 8.6 %collective-permute-start = (bf16[256,384]{0,1:T(8,128)(2,1)S(1)}, bf16[256,384]{0,1:T(8,128)(2,1)S(1)}, u32[]{:S(2)}, u32[]{:S(2)}) collective-permute-start(bf16[256,384]{0,1:T(8,128)(2,1)S(1)} %bitcast.79), channel_id=1, source_target_pairs={{0,4},{4,8},{8,12},{12,16},{16,20},{20,24},{24,28},{1,5},{5,9},{9,... | collective-permute-start | bytes 589832 | tf_op jit(solution)/shard_map/ppermute | solution.py:17
  26.7 26.0 %copy-start.35 = (f32[768]{0:T(1024)S(1)}, f32[768]{0:T(1024)}, u32[]{:S(2)}) copy-start(f32[768]{0:T(1024)} %param.23) | copy-start | bytes 9220
  26.7 61.6 %reduce-scatter.14.cloned.1.call-start = ((), (), s32[]{:S(2)}) async-start(), calls=%async_computation.9 | async-start | bytes 983040 | tf_op jit(solution)/shard_map/reduce_scatter | solution.py:161
  51.2 9.7 %copy-start.5 = (bf16[768,768]{1,0:T(8,128)(2,1)S(1)}, bf16[768,768]{1,0:T(8,128)(2,1)}, u32[]{:S(2)}) copy-start(bf16[768,768]{1,0:T(8,128)(2,1)} %param.25) | copy-start | bytes 3538948
  51.2 9.7 %copy-start.43 = (f32[768]{0:T(1024)S(1)}, f32[768]{0:T(1024)}, u32[]{:S(2)}) copy-start(f32[768]{0:T(1024)} %param.26) | copy-start | bytes 9220
  52.4 9.1 %copy-start.4 = (f32[64,768]{1,0:T(8,128)}, f32[64,768]{1,0:T(8,128)S(1)}, u32[]{:S(2)}) copy-start(f32[64,768]{1,0:T(8,128)S(1)} %get-tuple-element.36) | copy-start | bytes 589828
  52.6 8.8 %copy-start.8 = (f32[256,768]{1,0:T(8,128)S(1)}, f32[256,768]{1,0:T(8,128)}, u32[]{:S(2)}) copy-start(f32[256,768]{1,0:T(8,128)} %get-tuple-element.33) | copy-start | bytes 2359300
  65.0 49.1 %reduce-scatter.12.cloned.1.call-start = ((), (), s32[]{:S(2)}) async-start(), calls=%async_computation.8 | async-start | bytes 983040 | tf_op jit(solution)/shard_map/reduce_scatter | solution.py:144
  67.7 111.3 %all-reduce.11.cloned.1.call-start = ((), (), s32[]{:S(2)}) async-start(), calls=%async_computation.10 | async-start | bytes 1572864 | tf_op jit(solution)/shard_map/psum | solution.py:211
  114.1 11.7 %copy-start.25 = (bf16[192,768]{1,0:T(8,128)(2,1)S(1)}, bf16[192,768]{1,0:T(8,128)(2,1)}, u32[]{:S(2)}) copy-start(bf16[192,768]{1,0:T(8,128)(2,1)} %param.21) | copy-start | bytes 884740
  114.1 12.0 %copy-start.23 = (bf16[256,3,64]{0,2,1:T(8,128)(2,1)S(1)}, bf16[256,3,64]{0,2,1:T(8,128)(2,1)}, u32[]{:S(2)}) copy-start(bf16[256,3,64]{0,2,1:T(8,128)(2,1)} %copy-done.21) | copy-start | bytes 294916
  114.1 12.0 %copy-start.28 = (bf16[256,3,64]{0,2,1:T(8,128)(2,1)S(1)}, bf16[256,3,64]{0,2,1:T(8,128)(2,1)}, u32[]{:S(2)}) copy-start(bf16[256,3,64]{0,2,1:T(8,128)(2,1)} %copy-done.27) | copy-start | bytes 294916
  116.2 9.9 %copy-start.17 = (f32[64,768]{1,0:T(8,128)}, f32[64,768]{1,0:T(8,128)S(1)}, u32[]{:S(2)}) copy-start(f32[64,768]{1,0:T(8,128)S(1)} %get-tuple-element.41) | copy-start | bytes 589828
  127.6 4.4 copy-start.30
  127.6 4.3 copy-start.33
  128.9 12.5 %collective-permute-start.1 = (f32[256,384]{0,1:T(8,128)S(1)}, f32[256,384]{0,1:T(8,128)S(1)}, u32[]{:S(2)}, u32[]{:S(2)}) collective-permute-start(f32[256,384]{0,1:T(8,128)S(1)} %bitcast.73), channel_id=1, source_target_pairs={{4,0},{8,4},{12,8},{16,12},{20,16},{24,20},{28,24},{5,1},{9,5},{13... | collective-permute-start | bytes 1179656 | tf_op jit(solution)/shard_map/ppermute | solution.py:17
  132.3 9.1 %copy-start.14 = (f32[256,3,1,64]{0,3,1,2:T(8,128)}, f32[256,3,1,64]{0,3,1,2:T(8,128)S(1)}, u32[]{:S(2)}) copy-start(f32[256,3,1,64]{0,3,1,2:T(8,128)S(1)} %convolution_bitcast_fusion.3) | copy-start | bytes 589828
  132.3 10.7 %copy-start.31 = (bf16[768,576]{0,1:T(8,128)(2,1)S(1)}, bf16[768,576]{0,1:T(8,128)(2,1)}, u32[]{:S(2)}) copy-start(bf16[768,576]{0,1:T(8,128)(2,1)} %param.19) | copy-start | bytes 2654212
  144.5 99.4 %reduce-scatter.22.cloned.1.call-start = ((), (), s32[]{:S(2)}) async-start(), calls=%async_computation.14 | async-start | bytes 884736
  146.7 169.3 %reduce-scatter.18.cloned.1.call-start = ((), (), s32[]{:S(2)}) async-start(), calls=%async_computation.12 | async-start | bytes 2654208 | tf_op jit(solution)/shard_map/reduce_scatter | solution.py:224
  148.7 239.4 %reduce-scatter.20.cloned.1.call-start = ((), (), s32[]{:S(2)}) async-start(), calls=%async_computation.13 | async-start | bytes 2654208 | tf_op jit(solution)/shard_map/reduce_scatter | solution.py:226
  153.0 305.1 %reduce-scatter.16.cloned.1.call-start = ((), (), s32[]{:S(2)}) async-start(), calls=%async_computation.11 | async-start | bytes 2211840 | tf_op jit(solution)/shard_map/reduce_scatter | solution.py:218
  157.0 4.6 copy-start.38
  160.8 20.6 %copy-start.37 = (f32[768]{0:T(1024)S(1)}, f32[768]{0:T(1024)}, u32[]{:S(2)}) copy-start(f32[768]{0:T(1024)} %get-tuple-element.32) | copy-start | bytes 9220
  160.8 20.6 %copy-start.46 = (f32[768]{0:T(1024)S(1)}, f32[768]{0:T(1024)}, u32[]{:S(2)}) copy-start(f32[768]{0:T(1024)} %get-tuple-element.59) | copy-start | bytes 9220
  167.6 46.4 %copy-start.18 = (f32[64,768]{1,0:T(8,128)S(1)}, f32[64,768]{1,0:T(8,128)}, u32[]{:S(2)}) copy-start(f32[64,768]{1,0:T(8,128)} %copy-done.17) | copy-start | bytes 589828
  167.6 46.4 %copy-start.50 = (f32[64]{0:T(128)S(1)}, f32[64]{0:T(128)}, u32[]{:S(2)}) copy-start(f32[64]{0:T(128)} %dynamic-slice.22) | copy-start | bytes 772
  (29 other events, 41.6 us)
Sparse Core Ops, SparseCore 0:
  26.8 24.3 reduce-scatter.9
  65.1 23.0 reduce-scatter.13
  90.8 23.2 reduce-scatter.11
  144.6 34.3 all-reduce.10
  182.5 61.3 reduce-scatter.21
  247.8 68.0 reduce-scatter.17
  320.0 68.0 reduce-scatter.19
  392.2 65.9 reduce-scatter.15
where the time goes:
time: 469 us; the launch traced here: 465 us
  waiting for transfers between devices  325 us (69%)
  blocking collectives  49.2 us (10%)
  matrix products  25.1 us (5%)
  other arithmetic  21.6 us (5%)
  local copies, waits for them, and re-layouts  21.4 us (5%)
  between operations  16.2 us (3%)
  starting transfers between devices  6.5 us (1%)
    reduce_scatter x1, waiting for transfers between devices, per_device(): lax.psum_scatter(reduce_weight_grad, 'dp', scatter_dimension=1, tiled=True)  72.2 us
    reduce_scatter x1, waiting for transfers between devices, per_device(): lax.psum_scatter(expand_weight_grad, 'dp', scatter_dimension=0, tiled=True)  70.4 us
    reduce_scatter x1, waiting for transfers between devices, per_device(): lax.psum_scatter(input_weight_grad, 'dp', scatter_dimension=0, tiled=True)  70 us
    unnamed x9, waiting for transfers between devices  28.2 us
    unnamed x1, blocking collectives  27.8 us
    reduce_scatter x1, waiting for transfers between devices, per_device(): lax.psum_scatter(jnp.dot(activated, reduce_weight, preferred_element_type...  23.1 us
    reduce_scatter x1, waiting for transfers between devices, per_device(): lax.psum_scatter(jnp.dot(attended, output_weight, preferred_element_type=...  20.5 us
    reduce_scatter x1, waiting for transfers between devices, per_device(): lax.psum_scatter(jnp.einsum('rk,dk->rd', grad_pre16, expand_weight, prefe...  19.2 us
  transfers between devices with their start and end apart: 10, of which 10 were waited for; matrix products, arithmetic and copies ran while one was open for 8% of the time, Pallas kernels for 0%

commit v1 on v0

--- a/solution.py
+++ b/solution.py
@@ -1,6 +1,10 @@
+import functools
+
 import jax
 import jax.numpy as jnp
 from jax import lax
+from jax.experimental import pallas as pl
+from jax.experimental.pallas import tpu as pltpu
 from jax.sharding import PartitionSpec as P
 
 HEAD_DIM = 64
@@ -15,6 +19,117 @@
     count = lax.axis_size(axis)
     first, last = (max(0, -steps), min(count, count - steps))
     return lax.ppermute(value, axis, [(source, source + steps) for source in range(first, last)])
+
+
+def greet(axis, count):
+    me = lax.axis_index(axis)
+    barrier = pltpu.get_barrier_semaphore()
+
+    def signal(step, carry):
+        peer = lax.rem(me + step, count)
+        pl.semaphore_signal(
+            barrier, inc=1, device_id={axis: peer}, device_id_type=pl.DeviceIdType.MESH
+        )
+        return carry
+
+    lax.fori_loop(1, count, signal, 0)
+    pl.semaphore_wait(barrier, count - 1)
+    return me
+
+
+def scatter_kernel(axis, count, parts, *refs):
+    sources, results, landed = (refs[:parts], refs[parts : 2 * parts], refs[2 * parts : 3 * parts])
+    send_sem, recv_sem = refs[3 * parts :]
+    me = greet(axis, count)
+
+    def copy_of(step, part):
+        peer = lax.rem(me + step, count)
+        return pltpu.make_async_remote_copy(
+            src_ref=sources[part].at[peer],
+            dst_ref=landed[part].at[step - 1],
+            send_sem=send_sem.at[part, step - 1],
+            recv_sem=recv_sem.at[part, step - 1],
+            device_id={axis: peer},
+            device_id_type=pl.DeviceIdType.MESH,
+        )
+
+    def begin(step, carry):
+        for part in range(parts):
+            copy_of(step, part).start()
+        return carry
+
+    def finish(step, carry):
+        for part in range(parts):
+            copy_of(step, part).wait()
+        return carry
+
+    lax.fori_loop(1, count, begin, 0)
+    lax.fori_loop(1, count, finish, 0)
+    for part in range(parts):
+        total = sources[part][me].astype(jnp.float32)
+        for step in range(count - 1):
+            total = total + landed[part][step].astype(jnp.float32)
+        results[part][...] = total
+
+
+def scatter_sum(values, axis, identity):
+    count = values[0].shape[0]
+    parts = len(values)
+    vmem = pl.BlockSpec(memory_space=pltpu.VMEM)
+    return pl.pallas_call(
+        functools.partial(scatter_kernel, axis, count, parts),
+        out_shape=[jax.ShapeDtypeStruct(value.shape[1:], jnp.float32) for value in values],
+        in_specs=[vmem] * parts,
+        out_specs=[vmem] * parts,
+        scratch_shapes=[pltpu.VMEM((count - 1,) + value.shape[1:], value.dtype) for value in values]
+        + [pltpu.SemaphoreType.DMA((parts, count - 1)), pltpu.SemaphoreType.DMA((parts, count - 1))],
+        compiler_params=pltpu.CompilerParams(
+            collective_id=identity, has_side_effects=True, vmem_limit_bytes=40 * 1024 * 1024
+        ),
+    )(*values)
+
+
+def gather_kernel(axis, count, source, result, send_sem, recv_sem):
+    me = greet(axis, count)
+
+    def copy_of(step):
+        return pltpu.make_async_remote_copy(
+            src_ref=source,
+            dst_ref=result.at[me],
+            send_sem=send_sem.at[step - 1],
+            recv_sem=recv_sem.at[step - 1],
+            device_id={axis: lax.rem(me + step, count)},
+            device_id_type=pl.DeviceIdType.MESH,
+        )
+
+    def begin(step, carry):
+        copy_of(step).start()
+        return carry
+
+    def finish(step, carry):
+        copy_of(step).wait()
+        return carry
+
+    lax.fori_loop(1, count, begin, 0)
+    result[me] = source[...]
+    lax.fori_loop(1, count, finish, 0)
+
+
+def gather(value, axis, count, identity):
+    vmem = pl.BlockSpec(memory_space=pltpu.VMEM)
+    return pl.pallas_call(
+        functools.partial(gather_kernel, axis, count),
+        out_shape=jax.ShapeDtypeStruct((count,) + value.shape, value.dtype),
+        in_specs=[vmem],
+        out_specs=vmem,
+        scratch_shapes=[
+            pltpu.SemaphoreType.DMA((count - 1,)),
+            pltpu.SemaphoreType.DMA((count - 1,)),
+        ],
+        compiler_params=pltpu.CompilerParams(
+            collective_id=identity, has_side_effects=True, vmem_limit_bytes=40 * 1024 * 1024
+        ),
+    )(value)
 
 
 def layer_norm(values_in, gain_row, shift_row):
@@ -126,57 +241,40 @@
         .astype(b16)
         .reshape(block_rows, group_width)
     )
-    hidden_rows = (
-        own_rows(block_input)
-        + lax.psum_scatter(
-            jnp.dot(attended, output_weight, preferred_element_type=f32),
-            "tensor",
-            scatter_dimension=0,
-            tiled=True,
-        )
-        + output_bias
-    )
+    in_shares = (tensor_count, share_rows, block_input.shape[1])
+    (mixed_rows,) = scatter_sum(
+        [jnp.dot(attended, output_weight, preferred_element_type=f32).astype(b16).reshape(in_shares)],
+        "tensor",
+        0,
+    )
+    hidden_rows = own_rows(block_input) + mixed_rows + output_bias
     second_out, normed2, recip2 = layer_norm(hidden_rows, second_gain, second_shift)
-    second_in = lax.all_gather(second_out.astype(b16), "tensor", axis=0, tiled=True)
+    second_in = gather(second_out.astype(b16), "tensor", tensor_count, 1).reshape(block_input.shape)
     pre_act = jnp.dot(second_in, expand_weight, preferred_element_type=f32) + expand_bias
     activ, gelu_slope = gelu_parts(pre_act)
     activated = activ.astype(b16)
-    feed_rows = lax.psum_scatter(
-        jnp.dot(activated, reduce_weight, preferred_element_type=f32),
-        "tensor",
-        scatter_dimension=0,
-        tiled=True,
-    )
-    block_output = own_rows(live_col) * (hidden_rows + feed_rows + reduce_bias)
+    feed_part = jnp.dot(activated, reduce_weight, preferred_element_type=f32)
     grad_y = live_col * output_grad
     grad_y16 = grad_y.astype(b16)
-    reduce_weight_grad = jnp.einsum("rk,rd->kd", activated, grad_y16, preferred_element_type=f32)
-    reduce_bias_grad = jnp.sum(grad_y, axis=0)
     grad_pre = (
         jnp.einsum("rd,kd->rk", grad_y16, reduce_weight, preferred_element_type=f32) * gelu_slope
     )
     grad_pre16 = grad_pre.astype(b16)
-    expand_weight_grad = jnp.einsum("rd,rk->dk", second_in, grad_pre16, preferred_element_type=f32)
     expand_bias_grad = jnp.sum(grad_pre, axis=0)
-    grad_norm2 = lax.psum_scatter(
-        jnp.einsum("rk,dk->rd", grad_pre16, expand_weight, preferred_element_type=f32),
+    norm2_part = jnp.einsum("rk,dk->rd", grad_pre16, expand_weight, preferred_element_type=f32)
+    feed_rows, grad_norm2 = scatter_sum(
+        [feed_part.astype(b16).reshape(in_shares), norm2_part.astype(b16).reshape(in_shares)],
         "tensor",
-        scatter_dimension=0,
-        tiled=True,
-    )
-    back2, gain_part, shift_part = norm_back(grad_norm2, normed2, recip2, second_gain)
+        2,
+    )
+    block_output = own_rows(live_col) * (hidden_rows + feed_rows + reduce_bias)
+    back2, second_gain_part, second_shift_part = norm_back(grad_norm2, normed2, recip2, second_gain)
     grad_rows = own_rows(grad_y) + back2
-    gathered_hidden, part_sums = (
-        lax.all_gather(grad_rows, "tensor", axis=0, tiled=True),
-        lax.all_gather(jnp.stack([gain_part, shift_part], axis=0), "tensor", axis=0, tiled=True),
-    )
-    summed_parts = jnp.sum(part_sums.reshape(tensor_count, 2, part_sums.shape[1]), axis=0)
-    second_gain_grad = summed_parts[0]
-    second_shift_grad = summed_parts[1]
-    grad_hidden16 = gathered_hidden.astype(b16)
-    output_bias_grad = jnp.sum(gathered_hidden, axis=0)
+    grad_hidden16 = gather(grad_rows.astype(b16), "tensor", tensor_count, 3).reshape(
+        block_input.shape
+    )
     output_weight_grad = jnp.einsum(
-        "rk,rd->kd", attended, grad_hidden16, preferred_element_type=f32
+        "rd,rk->dk", grad_hidden16, attended, preferred_element_type=f32
     )
     grad_att = (
         jnp.einsum("rd,kd->rk", grad_hidden16, output_weight, preferred_element_type=f32)
@@ -194,7 +292,9 @@
     back_pair = jnp.concatenate([grad_keys[:block_rows], grad_values[:block_rows]], axis=1).reshape(
         block_rows, 2 * group_width
     )
-    from_next = from_behind(back_pair, "dp", -1).reshape(block_rows, 2 * group_heads, HEAD_DIM)
+    from_next = from_behind(back_pair.astype(b16), "dp", -1).reshape(
+        block_rows, 2 * group_heads, HEAD_DIM
+    )
     grad_mixed = jnp.stack(
         [
             grad_queries,
@@ -206,42 +306,71 @@
     bias_sums = jnp.sum(grad_mixed, axis=0)
     input_bias_grad = jnp.stack([bias_sums[:, 0], bias_sums[:, 2]], axis=1).reshape(2 * group_width)
     grad_mixed16 = grad_mixed.reshape(block_rows, 3 * group_width).astype(b16)
+    norm1_part = jnp.einsum("rc,dc->rd", grad_mixed16, input_weight, preferred_element_type=f32)
+    (grad_norm1,) = scatter_sum([norm1_part.astype(b16).reshape(in_shares)], "tensor", 4)
+    back1, first_gain_part, first_shift_part = norm_back(
+        grad_norm1, own_rows(normed1), own_rows(recip1), first_gain
+    )
+    input_grad = grad_rows + back1
     input_weight_grad = jnp.einsum("rd,rc->dc", first_in, grad_mixed16, preferred_element_type=f32)
-    norm1_part = jnp.einsum("rc,dc->rd", grad_mixed16, input_weight, preferred_element_type=f32)
-    grad_norm1 = lax.psum(norm1_part, "tensor")
-    back1, first_gain_grad, first_shift_grad = norm_back(grad_norm1, normed1, recip1, first_gain)
-    input_grad = grad_rows + own_rows(back1)
-    every_grad = tuple(
-        (
-            lax.psum_scatter(first_gain_grad, "dp", scatter_dimension=0, tiled=True),
-            lax.psum_scatter(first_shift_grad, "dp", scatter_dimension=0, tiled=True),
-            lax.psum_scatter(input_weight_grad, "dp", scatter_dimension=0, tiled=True),
-            lax.psum_scatter(input_bias_grad, "dp", scatter_dimension=0, tiled=True),
-            lax.psum_scatter(output_weight_grad, "dp", scatter_dimension=1, tiled=True),
-            lax.psum_scatter(output_bias_grad, "dp", scatter_dimension=0, tiled=True),
-            lax.psum_scatter(second_gain_grad, "dp", scatter_dimension=0, tiled=True),
-            lax.psum_scatter(second_shift_grad, "dp", scatter_dimension=0, tiled=True),
-            lax.psum_scatter(expand_weight_grad, "dp", scatter_dimension=0, tiled=True),
-            lax.psum_scatter(expand_bias_grad, "dp", scatter_dimension=0, tiled=True),
-            lax.psum_scatter(reduce_weight_grad, "dp", scatter_dimension=1, tiled=True),
-            lax.psum_scatter(reduce_bias_grad, "dp", scatter_dimension=0, tiled=True),
-        )
-    )
+    expand_weight_grad = jnp.einsum("rd,rk->dk", second_in, grad_pre16, preferred_element_type=f32)
+    reduce_weight_grad = jnp.einsum("rd,rk->dk", grad_y16, activated, preferred_element_type=f32)
+    shard_count = lax.axis_size("dp")
+
+    def pieces(value):
+        return value.reshape(shard_count, value.shape[0] // shard_count, value.shape[1])
+
+    wide = expand_bias_grad.shape[0] // shard_count
+    narrow = input_bias_grad.shape[0] // shard_count
+    vectors = jnp.stack(
+        [
+            value.reshape(shard_count, -1)
+            for value in (
+                first_gain_part,
+                first_shift_part,
+                jnp.sum(grad_rows, axis=0),
+                second_gain_part,
+                second_shift_part,
+                jnp.sum(own_rows(grad_y), axis=0),
+            )
+        ],
+        axis=1,
+    )
+    biases = jnp.stack(
+        [
+            expand_bias_grad.reshape(shard_count, wide),
+            jnp.pad(input_bias_grad.reshape(shard_count, narrow), ((0, 0), (0, wide - narrow))),
+        ],
+        axis=1,
+    )
+    input_sum, output_sum, expand_sum, reduce_sum, vector_sum, bias_sum = scatter_sum(
+        [
+            pieces(input_weight_grad.astype(b16)),
+            pieces(output_weight_grad.astype(b16)),
+            pieces(expand_weight_grad.astype(b16)),
+            pieces(reduce_weight_grad.astype(b16)),
+            vectors,
+            biases,
+        ],
+        "dp",
+        5,
+    )
+    vector_total = jnp.sum(gather(vector_sum, "tensor", tensor_count, 6), axis=0)
     return (
         block_output,
         input_grad,
-        every_grad[0],
-        every_grad[1],
-        every_grad[2],
-        every_grad[3],
-        every_grad[4],
-        every_grad[5],
-        every_grad[6],
-        every_grad[7],
-        every_grad[8],
-        every_grad[9],
-        every_grad[10],
-        every_grad[11],
+        vector_total[0],
+        vector_total[1],
+        input_sum,
+        bias_sum[1, :narrow],
+        output_sum.T,
+        vector_total[2],
+        vector_total[3],
+        vector_total[4],
+        expand_sum,
+        bias_sum[0],
+        reduce_sum.T,
+        vector_total[5],
     )
 
 

time: 469 us -> 198 us (0.42)
  waiting for transfers between devices: 325 us -> 0.76 us
  Pallas kernels: 0 us -> 130 us
  blocking collectives: 49.2 us -> 0 us
  between operations: 16.2 us -> 1.28 us
  matrix products: 25.1 us -> 14.6 us
  local copies, waits for them, and re-layouts: 21.4 us -> 27.3 us
    reduce_scatter x6 -> x0, waiting for transfers between devices: 275 us -> none  [the longest x1 72.2 us: per_device(): lax.psum_scatter(reduce_weight_grad, 'dp', scatter_dimension=1, tiled=True)]
    pallas_call x0 -> x7, Pallas kernels: none -> 130 us  [the longest x4 112 us: scatter_sum(): pl.pallas_call(functools.partial(scatter_kernel, axis, count, parts), out...]
    unnamed x9 -> x0, waiting for transfers between devices: 28.2 us -> none
    unnamed x1 -> x0, blocking collectives: 27.8 us -> none
    all_gather x3 -> x0, blocking collectives: 21.4 us -> none  [the longest x1 8.7 us: per_device(): lax.all_gather(grad_rows, 'tensor', axis=0, tiled=True)]
    ppermute x2, waiting for transfers between devices: 11.5 us -> 0.76 us  [from_behind(): lax.ppermute(value, axis, [(source, source + steps) for source in range(f...]
    psum x1 -> x0, waiting for transfers between devices: 9.87 us -> none  [per_device(): grad_norm1 = lax.psum(norm1_part, 'tensor')]
    another operation x3 -> x11, local copies, waits for them, and re-layouts: 1.96 us -> 8.09 us  [the longest x7 6.02 us: per_device(): jnp.stack([value.reshape(shard_count, -1) for value in (first_gain_part,...]
  transfers between devices with their start and end apart: 10 -> 2, of which waited for: 10 -> 1; matrix products, arithmetic and copies ran while one was open for 8% -> 7% of each run, Pallas kernels for 0% -> 0%
where the time goes in v1:
time: 198 us; the launch traced here: 196 us
  Pallas kernels  130 us (66%)
  local copies, waits for them, and re-layouts  27.3 us (14%)
  other arithmetic  17 us (9%)
  matrix products  14.6 us (7%)
  starting transfers between devices  5.19 us (3%)
    pallas_call x4, Pallas kernels, scatter_sum(): pl.pallas_call(functools.partial(scatter_kernel, axis, count, parts), out...  112 us
    pallas_call x3, Pallas kernels, gather(): pl.pallas_call(functools.partial(gather_kernel, axis, count), out_shape=j...  17.4 us
    unnamed x68, local copies, waits for them, and re-layouts  11.8 us
    another operation x7, local copies, waits for them, and re-layouts, per_device(): jnp.stack([value.reshape(shard_count, -1) for value in (first_gain_part,...  6.02 us
    ppermute x2, starting transfers between devices, from_behind(): lax.ppermute(value, axis, [(source, source + steps) for source in range(f...  5.19 us
  transfers between devices with their start and end apart: 2, of which 1 were waited for; matrix products, arithmetic and copies ran while one was open for 7% of the time, Pallas kernels for 0%

profile of v1, /device:TPU:9, one launch (start us, length us, event | category | flops | bytes accessed | tf_op | source)
XLA Modules:
  0.0 195.9 jit_solution(10485092145381713209)
XLA Ops:
  0.7 1.4 reduce_sum.171
  2.1 1.4 multiply_reduce_fusion.1
  4.0 1.6 fusion
  6.4 3.1 %collective-permute-start = (bf16[256,384]{0,1:T(8,128)(2,1)}, bf16[256,384]{0,1:T(8,128)(2,1)S(1)}, u32[]{:S(2)}, u32[]{:S(2)}) collective-permute-start(bf16[256,384]{0,1:T(8,128)(2,1)} %bitcast.4), channel_id=1, source_target_pairs={{0,4},{4,8},{8,12},{12,16},{16,20},{20,24},{24,28},{1,5},{5,9},{9,... | collective-permute-start | bytes 589832 | tf_op jit(solution)/shard_map/ppermute | solution.py:21
  13.2 1.3 broadcast_multiply_fusion
  17.2 8.3 %shard_map.263 = f32[64,768]{1,0:T(8,128)S(1)} custom-call(bf16[4,64,768]{2,1,0:T(8,128)(2,1)S(1)} %bitcast.99), custom_call_target="tpu_custom_call" | custom-call | tf_op jit(solution)/shard_map/pallas_call | solution.py:79
  25.9 6.7 %shard_map.264 = bf16[4,64,768]{2,1,0:T(8,128)(2,1)S(1)} custom-call(bf16[64,768]{1,0:T(8,128)(2,1)S(1)} %add_convert_fusion.1.source), custom_call_target="tpu_custom_call" | custom-call | tf_op jit(solution)/shard_map/pallas_call | solution.py:120
  33.8 1.3 fusion.34
  35.7 11.1 %shard_map.265 = (f32[64,768]{1,0:T(8,128)S(1)}, f32[64,768]{1,0:T(8,128)S(1)}) custom-call(bf16[4,64,768]{2,1,0:T(8,128)(2,1)S(1)} %bitcast.103, bf16[4,64,768]{2,1,0:T(8,128)(2,1)S(1)} %bitcast.100), custom_call_target="tpu_custom_call" | custom-call | tf_op jit(solution)/shard_map/pallas_call | solution.py:79
  47.0 1.4 fusion.26
  49.1 6.7 %shard_map.266 = bf16[4,64,768]{2,1,0:T(8,128)(2,1)S(1)} custom-call(bf16[64,768]{1,0:T(8,128)(2,1)S(1)} %convert_element_type.99.source), custom_call_target="tpu_custom_call" | custom-call | tf_op jit(solution)/shard_map/pallas_call | solution.py:120
  57.7 1.7 convolution_convert_fusion
  59.8 1.1 convolution_bitcast_fusion.1
  61.7 2.1 %collective-permute-start.1 = (bf16[256,384]{0,1:T(8,128)(2,1)}, bf16[256,384]{0,1:T(8,128)(2,1)}, u32[]{:S(2)}, u32[]{:S(2)}) collective-permute-start(bf16[256,384]{0,1:T(8,128)(2,1)} %bitcast.20), channel_id=1, source_target_pairs={{4,0},{8,4},{12,8},{16,12},{20,16},{24,20},{28,24},{5,1},{9,5},{13... | collective-permute-start | bytes 589832 | tf_op jit(solution)/shard_map/ppermute | solution.py:21
  63.8 1.0 convolution_convert_fusion.7
  64.7 1.3 stack_reshape.27
  66.1 1.3 stack_reshape.23
  69.4 1.9 copy.48
  71.3 1.3 convolution_bitcast_fusion.2
  72.6 1.1 fusion.15
  75.1 1.4 convolution_convert_fusion.2
  77.1 6.8 %shard_map.267 = f32[64,768]{1,0:T(8,128)S(1)} custom-call(bf16[4,64,768]{2,1,0:T(8,128)(2,1)S(1)} %bitcast.102), custom_call_target="tpu_custom_call" | custom-call | tf_op jit(solution)/shard_map/pallas_call | solution.py:79
  83.9 1.7 multiply_reduce_fusion.3
  86.9 1.6 copy.47
  89.2 1.4 stack.32.refs_4_
  90.6 1.0 copy-done.1
  91.6 1.3 copy-done.2
  93.6 86.3 %shard_map.268 = (f32[96,576]{1,0:T(8,128)S(1)}, f32[96,192]{1,0:T(8,128)S(1)}, f32[96,768]{1,0:T(8,128)S(1)}, f32[96,768]{1,0:T(8,128)S(1)}, f32[6,96]{1,0:T(8,128)S(1)}, /*index=5*/f32[2,96]{1,0:T(2,128)S(1)}) custom-call(bf16[8,96,576]{2,1,0:T(8,128)(2,1)S(1)} %bitcast.93, bf16[8,96,192]{2,1,0:T(8,128)(2,1)S(1)} %bitcast.98, ...), custom_call_target="tpu_custom_call" | custom-call | tf_op jit(solution)/shard_map/pallas_call | solution.py:79
  183.7 1.6 copy.50
  185.3 3.9 %shard_map.269 = f32[4,6,96]{2,1,0:T(8,128)S(1)} custom-call(f32[6,96]{1,0:T(8,128)S(1)} %get-tuple-element.24.source), custom_call_target="tpu_custom_call" | custom-call | tf_op jit(solution)/shard_map/pallas_call | solution.py:120
  191.1 1.8 multiply_add_fusion.1
  192.9 1.7 copy.57
  (131 shorter events, 27.3 us)
Async XLA Ops:
  0.6 32.6 %copy-start = (bf16[768,768]{1,0:T(8,128)(2,1)S(1)}, bf16[768,768]{1,0:T(8,128)(2,1)}, u32[]{:S(2)}) copy-start(bf16[768,768]{1,0:T(8,128)(2,1)} %param.27) | copy-start | bytes 3538948
  0.7 2.8 %copy-start.10 = (f32[256,768]{1,0:T(8,128)S(1)}, f32[256,768]{1,0:T(8,128)}, u32[]{:S(2)}) copy-start(f32[256,768]{1,0:T(8,128)} %param.16) | copy-start | bytes 2359300
  0.7 3.0 %copy-start.30 = (f32[384]{0:T(512)S(1)}, f32[384]{0:T(512)}, u32[]{:S(2)}) copy-start(f32[384]{0:T(512)} %param.20) | copy-start | bytes 4612
  0.7 3.3 %copy-start.21 = (f32[768]{0:T(1024)S(1)}, f32[768]{0:T(1024)}, u32[]{:S(2)}) copy-start(f32[768]{0:T(1024)} %param.17) | copy-start | bytes 9220
  0.7 3.3 %copy-start.27 = (f32[768]{0:T(1024)S(1)}, f32[768]{0:T(1024)}, u32[]{:S(2)}) copy-start(f32[768]{0:T(1024)} %param.18) | copy-start | bytes 9220
  3.6 9.5 %copy-start.11 = (f32[256,768]{1,0:T(8,128)}, f32[256,768]{1,0:T(8,128)S(1)}, u32[]{:S(2)}) copy-start(f32[256,768]{1,0:T(8,128)S(1)} %subtract_multiply_fusion) | copy-start | bytes 2359300
  3.7 5.9 %copy-start.29 = (s32[8]{0:T(128)S(1)}, s32[8]{0:T(128)}, u32[]{:S(2)}) copy-start(s32[8]{0:T(128)} %param.31) | copy-start | bytes 100
  5.6 9.6 %copy-start.19 = (bf16[256,576]{0,1:T(8,128)(2,1)}, bf16[256,576]{0,1:T(8,128)(2,1)S(1)}, u32[]{:S(2)}) copy-start(bf16[256,576]{0,1:T(8,128)(2,1)S(1)} %fusion) | copy-start | bytes 884740
  5.6 10.1 %copy-start.17 = (bf16[256,3,64]{0,2,1:T(8,128)(2,1)}, bf16[256,3,64]{0,2,1:T(8,128)(2,1)S(1)}, u32[]{:S(2)}) copy-start(bf16[256,3,64]{0,2,1:T(8,128)(2,1)S(1)} %get-tuple-element.86) | copy-start | bytes 294916
  6.4 8.8 %collective-permute-start = (bf16[256,384]{0,1:T(8,128)(2,1)}, bf16[256,384]{0,1:T(8,128)(2,1)S(1)}, u32[]{:S(2)}, u32[]{:S(2)}) collective-permute-start(bf16[256,384]{0,1:T(8,128)(2,1)} %bitcast.4), channel_id=1, source_target_pairs={{0,4},{4,8},{8,12},{12,16},{16,20},{20,24},{24,28},{1,5},{5,9},{9,... | collective-permute-start | bytes 589832 | tf_op jit(solution)/shard_map/ppermute | solution.py:21
  15.2 1.1 copy-start.18
  15.8 1.1 copy-start.16
  16.3 9.1 %copy-start.23 = (f32[768]{0:T(1024)S(1)}, f32[768]{0:T(1024)}, u32[]{:S(2)}) copy-start(f32[768]{0:T(1024)} %param.22) | copy-start | bytes 9220
  16.3 9.5 %copy-start.20 = (f32[768]{0:T(1024)S(1)}, f32[768]{0:T(1024)}, u32[]{:S(2)}) copy-start(f32[768]{0:T(1024)} %param.23) | copy-start | bytes 9220
  16.4 9.5 %copy-start.24 = (f32[768]{0:T(1024)S(1)}, f32[768]{0:T(1024)}, u32[]{:S(2)}) copy-start(f32[768]{0:T(1024)} %param.24) | copy-start | bytes 9220
  16.9 15.8 %copy-start.13 = (bf16[768,768]{1,0:T(8,128)(2,1)S(1)}, bf16[768,768]{1,0:T(8,128)(2,1)}, u32[]{:S(2)}) copy-start(bf16[768,768]{1,0:T(8,128)(2,1)} %param.25) | copy-start | bytes 3538948
  16.9 15.8 %copy-start.25 = (f32[768]{0:T(1024)S(1)}, f32[768]{0:T(1024)}, u32[]{:S(2)}) copy-start(f32[768]{0:T(1024)} %param.26) | copy-start | bytes 9220
  35.2 11.9 %copy-start.26 = (f32[768]{0:T(1024)S(1)}, f32[768]{0:T(1024)}, u32[]{:S(2)}) copy-start(f32[768]{0:T(1024)} %param.28) | copy-start | bytes 9220
  57.2 2.2 %copy-start.15 = (f32[512,3,64]{0,2,1:T(8,128)}, f32[512,3,64]{0,2,1:T(8,128)S(1)}, u32[]{:S(2)}) copy-start(f32[512,3,64]{0,2,1:T(8,128)S(1)} %convolution_bitcast_fusion) | copy-start | bytes 1179652
  61.7 10.9 %collective-permute-start.1 = (bf16[256,384]{0,1:T(8,128)(2,1)}, bf16[256,384]{0,1:T(8,128)(2,1)}, u32[]{:S(2)}, u32[]{:S(2)}) collective-permute-start(bf16[256,384]{0,1:T(8,128)(2,1)} %bitcast.20), channel_id=1, source_target_pairs={{4,0},{8,4},{12,8},{16,12},{20,16},{24,20},{28,24},{5,1},{9,5},{13... | collective-permute-start | bytes 589832 | tf_op jit(solution)/shard_map/ppermute | solution.py:21
  72.6 1.4 copy-start.31
  73.9 1.1 copy-start.12
  73.9 1.1 copy-start.28
  86.9 2.3 %copy-start.22 = (f32[8,1,96]{2,1,0:T(1,128)S(1)}, f32[8,1,96]{2,1,0:T(1,128)}, u32[]{:S(2)}) copy-start(f32[8,1,96]{2,1,0:T(1,128)} %stack_reshape.21) | copy-start | bytes 9220
  90.6 1.0 copy-start.1
  91.6 1.3 copy-start.2
  92.9 0.8 copy-start.8
  179.9 0.7 copy-start.3
  180.6 0.7 copy-start.5
  181.3 0.7 copy-start.7
  182.7 11.8 %copy-start.6 = (f32[96,768]{1,0:T(8,128)S(1)}, f32[96,768]{1,0:T(8,128)}, u32[]{:S(2)}) copy-start(f32[96,768]{1,0:T(8,128)} %copy-done.5) | copy-start | bytes 884740
  182.7 12.5 %copy-start.4 = (f32[96,768]{1,0:T(8,128)S(1)}, f32[96,768]{1,0:T(8,128)}, u32[]{:S(2)}) copy-start(f32[96,768]{1,0:T(8,128)} %copy-done.3) | copy-start | bytes 884740
  (2 other events, 1.3 us)

commit v2 on v1

--- a/solution.py
+++ b/solution.py
@@ -132,21 +132,361 @@
     )(value)
 
 
+def across(left, right, left_dim, right_dim):
+    return lax.dot_general(
+        left, right, (((left_dim,), (right_dim,)), ((), ())), preferred_element_type=jnp.float32
+    )
+
+
+def norm_back_rows(grad_in, normed, reciprocal, gain_row):
+    scaled = grad_in * gain_row
+    spread = (
+        scaled
+        - jnp.mean(scaled, axis=-1, keepdims=True)
+        - normed * jnp.mean(scaled * normed, axis=-1, keepdims=True)
+    )
+    return (
+        reciprocal * spread,
+        jnp.sum(grad_in * normed, axis=0, keepdims=True),
+        jnp.sum(grad_in, axis=0, keepdims=True),
+    )
+
+
+def tail_kernel(
+    shards,
+    groups,
+    heads,
+    feed_ref,
+    norm2_ref,
+    expand_ref,
+    reduce_ref,
+    hidden_ref,
+    normed2_ref,
+    recip2_ref,
+    gain2_ref,
+    reduce_bias_ref,
+    grad_y_ref,
+    live_ref,
+    expand_bias_ref,
+    attended_ref,
+    output_weight_ref,
+    query_ref,
+    key_ref,
+    value_ref,
+    soft_ref,
+    first_in_ref,
+    input_weight_ref,
+    normed1_ref,
+    recip1_ref,
+    gain1_ref,
+    block_out,
+    input_out,
+    input_sum,
+    output_sum,
+    expand_sum,
+    reduce_sum,
+    vector_sum,
+    norm2_land,
+    feed_land,
+    rows16,
+    rows_all,
+    norm1_part,
+    norm1_land,
+    vector_part,
+    vector_land,
+    vector_own,
+    vector_far,
+    back_own,
+    back_land,
+    mixed_grad,
+    output_part,
+    input_part,
+    expand_land,
+    reduce_land,
+    output_land,
+    input_land,
+    tensor_send,
+    tensor_recv,
+    dp_send,
+    dp_recv,
+    back_send,
+    back_recv,
+):
+    f32 = jnp.float32
+    b16 = jnp.bfloat16
+    mesh_id = pl.DeviceIdType.MESH
+    my_shard = lax.axis_index("dp")
+    my_group = lax.axis_index("tensor")
+    barrier = pltpu.get_barrier_semaphore()
+
+    def signal_dp(step, carry):
+        pl.semaphore_signal(
+            barrier, inc=1, device_id={"dp": lax.rem(my_shard + step, shards)}, device_id_type=mesh_id
+        )
+        return carry
+
+    def signal_tensor(step, carry):
+        pl.semaphore_signal(
+            barrier,
+            inc=1,
+            device_id={"tensor": lax.rem(my_group + step, groups)},
+            device_id_type=mesh_id,
+        )
+        return carry
+
+    lax.fori_loop(1, groups, signal_tensor, 0)
+    lax.fori_loop(1, shards, signal_dp, 0)
+    pl.semaphore_wait(barrier, shards + groups - 2)
+
+    def tensor_copy(kind, source, target, step):
+        peer = lax.rem(my_group + step, groups)
+        return pltpu.make_async_remote_copy(
+            src_ref=source(peer),
+            dst_ref=target(step),
+            send_sem=tensor_send.at[kind, step - 1],
+            recv_sem=tensor_recv.at[kind, step - 1],
+            device_id={"tensor": peer},
+            device_id_type=mesh_id,
+        )
+
+    def dp_copy(kind, source, target, step):
+        peer = lax.rem(my_shard + step, shards)
+        return pltpu.make_async_remote_copy(
+            src_ref=source(peer),
+            dst_ref=target.at[step - 1],
+            send_sem=dp_send.at[kind, step - 1],
+            recv_sem=dp_recv.at[kind, step - 1],
+            device_id={"dp": peer},
+            device_id_type=mesh_id,
+        )
+
+    def begin(copy, kind, source, target, count):
+        def run(step, carry):
+            copy(kind, source, target, step).start()
+            return carry
+
+        lax.fori_loop(1, count, run, 0)
+
+    def finish(copy, kind, source, target, count):
+        def run(step, carry):
+            copy(kind, source, target, step).wait()
+            return carry
+
+        lax.fori_loop(1, count, run, 0)
+
+    norm2_move = (tensor_copy, 0, lambda p: norm2_ref.at[p], lambda t: norm2_land.at[t - 1], groups)
+    feed_move = (tensor_copy, 1, lambda p: feed_ref.at[p], lambda t: feed_land.at[t - 1], groups)
+    rows_move = (tensor_copy, 2, lambda p: rows16, lambda t: rows_all.at[my_group], groups)
+    norm1_move = (tensor_copy, 3, lambda p: norm1_part.at[p], lambda t: norm1_land.at[t - 1], groups)
+    vector_move = (tensor_copy, 4, lambda p: vector_part, lambda t: vector_land.at[t - 1], groups)
+    reduce_move = (dp_copy, 0, lambda p: reduce_ref.at[p], reduce_land, shards)
+    expand_move = (dp_copy, 1, lambda p: expand_ref.at[p], expand_land, shards)
+    output_move = (dp_copy, 2, lambda p: output_part.at[p], output_land, shards)
+    input_move = (dp_copy, 3, lambda p: input_part.at[p], input_land, shards)
+    far_move = (dp_copy, 4, lambda p: vector_own, vector_far, shards)
+
+    def total_of(own, land, count):
+        total = own.astype(f32)
+        for step in range(count - 1):
+            total = total + land[step].astype(f32)
+        return total
+
+    begin(*norm2_move)
+    begin(*reduce_move)
+    begin(*feed_move)
+    vector_part[...] = jnp.zeros_like(vector_part)
+    finish(*norm2_move)
+    grad_norm2 = total_of(norm2_ref[my_group], norm2_land, groups)
+    back2, gain_row, shift_row = norm_back_rows(
+        grad_norm2, normed2_ref[...], recip2_ref[...], gain2_ref[...]
+    )
+    grad_y = grad_y_ref[...]
+    grad_rows = grad_y + back2
+    rows16[...] = grad_rows.astype(b16)
+    begin(*rows_move)
+    input_out[...] = grad_rows
+    rows_all[my_group] = grad_rows.astype(b16)
+    width = grad_y.shape[1]
+    vector_part[2:3, :width] = jnp.sum(grad_rows, axis=0, keepdims=True)
+    vector_part[3:4, :width] = gain_row
+    vector_part[4:5, :width] = shift_row
+    vector_part[5:6, :width] = jnp.sum(grad_y, axis=0, keepdims=True)
+    vector_part[6:7, : expand_bias_ref.shape[1]] = expand_bias_ref[...]
+    finish(*feed_move)
+    feed_rows = total_of(feed_ref[my_group], feed_land, groups)
+    block_out[...] = live_ref[...] * (hidden_ref[...] + feed_rows + reduce_bias_ref[...])
+    finish(*rows_move)
+    share = rows_all.shape[1]
+    rows = groups * share
+    hidden16 = rows_all[...].reshape(rows, width)
+    grad_att = across(hidden16, output_weight_ref[...], 1, 1).astype(b16)
+    scale = HEAD_DIM ** (-0.5)
+    span = heads * HEAD_DIM
+    for head in range(heads):
+        low = head * HEAD_DIM
+        high = low + HEAD_DIM
+        first = 3 * low
+        att = grad_att[:, low:high]
+        keys = key_ref[:, low:high]
+        soft = soft_ref[head]
+        grad_soft = across(att, value_ref[:, low:high], 1, 1)
+        delta = jnp.sum(soft * grad_soft, axis=-1, keepdims=True)
+        grad_scores = (scale * soft * (grad_soft - delta)).astype(b16)
+        grad_keys = across(grad_scores, query_ref[:, low:high], 0, 0)
+        grad_values = across(soft.astype(b16), att, 0, 0)
+        back_own[:, low:high] = grad_keys[:rows].astype(b16)
+        back_own[:, span + low : span + high] = grad_values[:rows].astype(b16)
+        mixed_grad[:, first : first + HEAD_DIM] = across(grad_scores, keys, 1, 0)
+        mixed_grad[:, first + HEAD_DIM : first + 2 * HEAD_DIM] = grad_keys[rows:]
+        mixed_grad[:, first + 2 * HEAD_DIM : first + 3 * HEAD_DIM] = grad_values[rows:]
+
+    back_copy = pltpu.make_async_remote_copy(
+        src_ref=back_own,
+        dst_ref=back_land,
+        send_sem=back_send,
+        recv_sem=back_recv,
+        device_id={"dp": lax.rem(my_shard + shards - 1, shards)},
+        device_id_type=mesh_id,
+    )
+
+    @pl.when(my_shard > 0)
+    def _():
+        back_copy.start()
+
+    begin(*expand_move)
+    output_grad = across(hidden16, attended_ref[...], 0, 0)
+    piece = output_part.shape[1]
+    for part in range(shards):
+        output_part[part] = output_grad[part * piece : (part + 1) * piece].astype(b16)
+    begin(*output_move)
+
+    @pl.when(my_shard < shards - 1)
+    def _():
+        back_copy.wait_recv()
+
+    @pl.when(my_shard == shards - 1)
+    def _():
+        back_land[...] = jnp.zeros_like(back_land)
+
+    for head in range(heads):
+        low = head * HEAD_DIM
+        high = low + HEAD_DIM
+        key_at = 3 * low + HEAD_DIM
+        value_at = key_at + HEAD_DIM
+        mixed_grad[:, key_at:value_at] += back_land[:, low:high].astype(f32)
+        mixed_grad[:, value_at : value_at + HEAD_DIM] += back_land[
+            :, span + low : span + high
+        ].astype(f32)
+    mixed = mixed_grad[...]
+    mixed16 = mixed.astype(b16)
+    norm1 = across(mixed16, input_weight_ref[...], 1, 1).astype(b16)
+    norm1_part[...] = norm1.reshape(groups, share, width)
+    begin(*norm1_move)
+    input_grad = across(first_in_ref[...], mixed16, 0, 0)
+    for part in range(shards):
+        input_part[part] = input_grad[part * piece : (part + 1) * piece].astype(b16)
+    begin(*input_move)
+    vector_part[7:8, : mixed.shape[1]] = jnp.sum(mixed, axis=0, keepdims=True)
+    finish(*norm1_move)
+    grad_norm1 = total_of(norm1_part[my_group], norm1_land, groups)
+    back1, gain_row, shift_row = norm_back_rows(
+        grad_norm1, normed1_ref[...], recip1_ref[...], gain1_ref[...]
+    )
+    vector_part[0:1, :width] = gain_row
+    vector_part[1:2, :width] = shift_row
+    begin(*vector_move)
+    input_out[...] += back1
+    finish(*vector_move)
+    own = vector_part[...]
+    added = vector_land[0]
+    for step in range(1, groups - 1):
+        added = added + vector_land[step]
+    row_index = lax.broadcasted_iota(jnp.int32, own.shape, 0)
+    vector_own[...] = own + jnp.where(row_index < 6, added, 0.0)
+    begin(*far_move)
+
+    @pl.when(my_shard > 0)
+    def _():
+        back_copy.wait_send()
+
+    finish(*reduce_move)
+    reduce_sum[...] = total_of(reduce_ref[my_shard], reduce_land, shards)
+    finish(*expand_move)
+    expand_sum[...] = total_of(expand_ref[my_shard], expand_land, shards)
+    finish(*output_move)
+    output_sum[...] = total_of(output_part[my_shard], output_land, shards)
+    finish(*input_move)
+    input_sum[...] = total_of(input_part[my_shard], input_land, shards)
+    finish(*far_move)
+    vector_sum[...] = total_of(vector_own[...], vector_far, shards)
+
+
+def tail(shards, groups, heads, operands):
+    f32 = jnp.float32
+    b16 = jnp.bfloat16
+    share, width = operands[4].shape
+    rows = share * groups
+    piece = operands[2].shape[1]
+    hidden = operands[2].shape[2]
+    span = heads * HEAD_DIM
+    broad = max(width, hidden, 3 * span)
+    vmem = pl.BlockSpec(memory_space=pltpu.VMEM)
+
+    def shape(*sizes):
+        return jax.ShapeDtypeStruct(sizes, f32)
+
+    dma = pltpu.SemaphoreType.DMA
+    return pl.pallas_call(
+        functools.partial(tail_kernel, shards, groups, heads),
+        out_shape=[
+            shape(share, width),
+            shape(share, width),
+            shape(piece, 3 * span),
+            shape(piece, span),
+            shape(piece, hidden),
+            shape(piece, hidden),
+            shape(8, broad),
+        ],
+        in_specs=[vmem] * len(operands),
+        out_specs=[vmem] * 7,
+        scratch_shapes=[
+            pltpu.VMEM((groups - 1, share, width), b16),
+            pltpu.VMEM((groups - 1, share, width), b16),
+            pltpu.VMEM((share, width), b16),
+            pltpu.VMEM((groups, share, width), b16),
+            pltpu.VMEM((groups, share, width), b16),
+            pltpu.VMEM((groups - 1, share, width), b16),
+            pltpu.VMEM((8, broad), f32),
+            pltpu.VMEM((groups - 1, 8, broad), f32),
+            pltpu.VMEM((8, broad), f32),
+            pltpu.VMEM((shards - 1, 8, broad), f32),
+            pltpu.VMEM((rows, 2 * span), b16),
+            pltpu.VMEM((rows, 2 * span), b16),
+            pltpu.VMEM((rows, 3 * span), f32),
+            pltpu.VMEM((shards, piece, span), b16),
+            pltpu.VMEM((shards, piece, 3 * span), b16),
+            pltpu.VMEM((shards - 1, piece, hidden), b16),
+            pltpu.VMEM((shards - 1, piece, hidden), b16),
+            pltpu.VMEM((shards - 1, piece, span), b16),
+            pltpu.VMEM((shards - 1, piece, 3 * span), b16),
+            dma((5, groups - 1)),
+            dma((5, groups - 1)),
+            dma((5, shards - 1)),
+            dma((5, shards - 1)),
+            dma,
+            dma,
+        ],
+        compiler_params=pltpu.CompilerParams(
+            collective_id=2, has_side_effects=True, vmem_limit_bytes=48 * 1024 * 1024
+        ),
+    )(*operands)
+
+
 def layer_norm(values_in, gain_row, shift_row):
     centred = values_in - jnp.mean(values_in, axis=-1, keepdims=True)
     reciprocal = lax.rsqrt(jnp.mean(centred * centred, axis=-1, keepdims=True) + EPSILON)
     normed = centred * reciprocal
     return (normed * gain_row + shift_row, normed, reciprocal)
-
-
-def norm_back(grad_in, normed, reciprocal, gain_row):
-    scaled = grad_in * gain_row
-    spread = (
-        scaled
-        - jnp.mean(scaled, axis=-1, keepdims=True)
-        - normed * jnp.mean(scaled * normed, axis=-1, keepdims=True)
-    )
-    return (reciprocal * spread, jnp.sum(grad_in * normed, axis=0), jnp.sum(grad_in, axis=0))
 
 
 def gelu_parts(pre_act):
@@ -235,7 +575,8 @@
     scores = masked_scores(queries, key_rows, allowed)
     row_top = jnp.max(scores, axis=-1, keepdims=True)
     logsum = row_top + jnp.log(jnp.sum(jnp.exp(scores - row_top), axis=-1, keepdims=True))
-    soft16 = jnp.exp(scores - logsum).astype(b16)
+    soft = jnp.exp(scores - logsum)
+    soft16 = soft.astype(b16)
     attended = (
         jnp.einsum("hqk,khd->qhd", soft16, value_rows, preferred_element_type=f32)
         .astype(b16)
@@ -262,113 +603,70 @@
     grad_pre16 = grad_pre.astype(b16)
     expand_bias_grad = jnp.sum(grad_pre, axis=0)
     norm2_part = jnp.einsum("rk,dk->rd", grad_pre16, expand_weight, preferred_element_type=f32)
-    feed_rows, grad_norm2 = scatter_sum(
-        [feed_part.astype(b16).reshape(in_shares), norm2_part.astype(b16).reshape(in_shares)],
-        "tensor",
-        2,
-    )
-    block_output = own_rows(live_col) * (hidden_rows + feed_rows + reduce_bias)
-    back2, second_gain_part, second_shift_part = norm_back(grad_norm2, normed2, recip2, second_gain)
-    grad_rows = own_rows(grad_y) + back2
-    grad_hidden16 = gather(grad_rows.astype(b16), "tensor", tensor_count, 3).reshape(
-        block_input.shape
-    )
-    output_weight_grad = jnp.einsum(
-        "rd,rk->dk", grad_hidden16, attended, preferred_element_type=f32
-    )
-    grad_att = (
-        jnp.einsum("rd,kd->rk", grad_hidden16, output_weight, preferred_element_type=f32)
-        .astype(b16)
-        .reshape(block_rows, group_heads, HEAD_DIM)
-    )
-    scores = masked_scores(queries, key_rows, allowed)
-    soft = jnp.exp(scores - logsum)
-    grad_soft = jnp.einsum("qhd,khd->hqk", grad_att, value_rows, preferred_element_type=f32)
-    delta = jnp.sum(soft * grad_soft, axis=-1, keepdims=True)
-    grad_scores = (score_scale * soft * (grad_soft - delta)).astype(b16)
-    grad_queries = jnp.einsum("hqk,khd->qhd", grad_scores, key_rows, preferred_element_type=f32)
-    grad_keys = jnp.einsum("hqk,qhd->khd", grad_scores, queries, preferred_element_type=f32)
-    grad_values = jnp.einsum("hqk,qhd->khd", soft.astype(b16), grad_att, preferred_element_type=f32)
-    back_pair = jnp.concatenate([grad_keys[:block_rows], grad_values[:block_rows]], axis=1).reshape(
-        block_rows, 2 * group_width
-    )
-    from_next = from_behind(back_pair.astype(b16), "dp", -1).reshape(
-        block_rows, 2 * group_heads, HEAD_DIM
-    )
-    grad_mixed = jnp.stack(
-        [
-            grad_queries,
-            grad_keys[block_rows:] + from_next[:, :group_heads],
-            grad_values[block_rows:] + from_next[:, group_heads:],
-        ],
-        axis=2,
-    )
-    bias_sums = jnp.sum(grad_mixed, axis=0)
-    input_bias_grad = jnp.stack([bias_sums[:, 0], bias_sums[:, 2]], axis=1).reshape(2 * group_width)
-    grad_mixed16 = grad_mixed.reshape(block_rows, 3 * group_width).astype(b16)
-    norm1_part = jnp.einsum("rc,dc->rd", grad_mixed16, input_weight, preferred_element_type=f32)
-    (grad_norm1,) = scatter_sum([norm1_part.astype(b16).reshape(in_shares)], "tensor", 4)
-    back1, first_gain_part, first_shift_part = norm_back(
-        grad_norm1, own_rows(normed1), own_rows(recip1), first_gain
-    )
-    input_grad = grad_rows + back1
-    input_weight_grad = jnp.einsum("rd,rc->dc", first_in, grad_mixed16, preferred_element_type=f32)
+    shard_count = lax.axis_size("dp")
     expand_weight_grad = jnp.einsum("rd,rk->dk", second_in, grad_pre16, preferred_element_type=f32)
     reduce_weight_grad = jnp.einsum("rd,rk->dk", grad_y16, activated, preferred_element_type=f32)
-    shard_count = lax.axis_size("dp")
 
     def pieces(value):
         return value.reshape(shard_count, value.shape[0] // shard_count, value.shape[1])
 
-    wide = expand_bias_grad.shape[0] // shard_count
-    narrow = input_bias_grad.shape[0] // shard_count
-    vectors = jnp.stack(
+    def two_rows(values):
+        return values.reshape(values.shape[0], group_width)
+
+    block_output, input_grad, input_sum, output_sum, expand_sum, reduce_sum, vectors = tail(
+        shard_count,
+        tensor_count,
+        group_heads,
         [
-            value.reshape(shard_count, -1)
-            for value in (
-                first_gain_part,
-                first_shift_part,
-                jnp.sum(grad_rows, axis=0),
-                second_gain_part,
-                second_shift_part,
-                jnp.sum(own_rows(grad_y), axis=0),
-            )
-        ],
-        axis=1,
-    )
-    biases = jnp.stack(
-        [
-            expand_bias_grad.reshape(shard_count, wide),
-            jnp.pad(input_bias_grad.reshape(shard_count, narrow), ((0, 0), (0, wide - narrow))),
-        ],
-        axis=1,
-    )
-    input_sum, output_sum, expand_sum, reduce_sum, vector_sum, bias_sum = scatter_sum(
-        [
-            pieces(input_weight_grad.astype(b16)),
-            pieces(output_weight_grad.astype(b16)),
+            feed_part.astype(b16).reshape(in_shares),
+            norm2_part.astype(b16).reshape(in_shares),
             pieces(expand_weight_grad.astype(b16)),
             pieces(reduce_weight_grad.astype(b16)),
-            vectors,
-            biases,
+            hidden_rows,
+            normed2,
+            recip2,
+            second_gain[None],
+            reduce_bias[None],
+            own_rows(grad_y),
+            own_rows(live_col),
+            expand_bias_grad[None],
+            attended,
+            output_weight,
+            two_rows(queries),
+            two_rows(key_rows),
+            two_rows(value_rows),
+            soft,
+            first_in,
+            input_weight,
+            own_rows(normed1),
+            own_rows(recip1),
+            first_gain[None],
         ],
-        "dp",
-        5,
-    )
-    vector_total = jnp.sum(gather(vector_sum, "tensor", tensor_count, 6), axis=0)
+    )
+    features = block_input.shape[1]
+    bias_pairs = vectors[7, : 3 * group_width].reshape(group_heads, 3, HEAD_DIM)
+    input_bias_grad = jnp.stack([bias_pairs[:, 0], bias_pairs[:, 2]], axis=1).reshape(
+        2 * group_width
+    )
+
+    def own_piece(value):
+        size = value.shape[-1] // shard_count
+        return lax.dynamic_slice_in_dim(value, shard_index * size, size, value.ndim - 1)
+
+    vector_total = own_piece(vectors[:6, :features])
     return (
         block_output,
         input_grad,
         vector_total[0],
         vector_total[1],
         input_sum,
-        bias_sum[1, :narrow],
+        own_piece(input_bias_grad),
         output_sum.T,
         vector_total[2],
         vector_total[3],
         vector_total[4],
         expand_sum,
-        bias_sum[0],
+        own_piece(vectors[6, : expand_bias_grad.shape[0]]),
         reduce_sum.T,
         vector_total[5],
     )

time: 198 us -> 179 us (0.904)
  Pallas kernels: 130 us -> 109 us
  local copies, waits for them, and re-layouts: 27.3 us -> 40.6 us
  other arithmetic: 17 us -> 12 us
  matrix products: 14.6 us -> 10.2 us
  starting transfers between devices: 5.19 us -> 3.11 us
    pallas_call x4 -> x1, Pallas kernels: 112 us -> 7.65 us  [scatter_sum(): pl.pallas_call(functools.partial(scatter_kernel, axis, count, parts), out...]
    pallas_call x0 -> x1, Pallas kernels: none -> 94.3 us  [tail(): pl.pallas_call(functools.partial(tail_kernel, shards, groups, heads), out...]
    pallas_call x3 -> x1, Pallas kernels: 17.4 us -> 6.71 us  [gather(): pl.pallas_call(functools.partial(gather_kernel, axis, count), out_shape=j...]
    unnamed x68 -> x77, local copies, waits for them, and re-layouts: 11.8 us -> 21.2 us
    concatenate x0 -> x4, local copies, waits for them, and re-layouts: none -> 6.59 us  [the longest x2 3.31 us: per_device(): jnp.concatenate([prior_pair[:, group_heads:], mixed[:, :, 2]], axis=0)]
    dot_general x8 -> x0, matrix products: 6.57 us -> none  [the longest x1 1.38 us: per_device(): jnp.einsum('rd,rc->dc', first_in, grad_mixed16, preferred_element_type=f32)]
    another operation x12 -> x2, local copies, waits for them, and re-layouts: 8.1 us -> 1.73 us  [the longest x1 1.65 us: two_rows(): return values.reshape(values.shape[0], group_width)]
    dynamic_slice x0 -> x9, local copies, waits for them, and re-layouts: none -> 4.59 us  [the longest x6 2.66 us: own_rows(): return lax.dynamic_slice_in_dim(values, row_start, share_rows, 0)]
  transfers between devices with their start and end apart: 2 -> 1, of which waited for: 1 -> 0; matrix products, arithmetic and copies ran while one was open for 7% -> 8% of each run, Pallas kernels for 0% -> 0%
where the time goes in v2:
time: 179 us; the launch traced here: 176 us
  Pallas kernels  109 us (61%)
  local copies, waits for them, and re-layouts  40.6 us (23%)
  other arithmetic  12 us (7%)
  matrix products  10.2 us (6%)
  starting transfers between devices  3.11 us (2%)
    pallas_call x1, Pallas kernels, tail(): pl.pallas_call(functools.partial(tail_kernel, shards, groups, heads), out...  94.3 us
    unnamed x77, local copies, waits for them, and re-layouts  21.2 us
    pallas_call x1, Pallas kernels, scatter_sum(): pl.pallas_call(functools.partial(scatter_kernel, axis, count, parts), out...  7.65 us
    pallas_call x1, Pallas kernels, gather(): pl.pallas_call(functools.partial(gather_kernel, axis, count), out_shape=j...  6.71 us
  transfers between devices with their start and end apart: 1, of which 0 were waited for; matrix products, arithmetic and copies ran while one was open for 8% of the time, Pallas kernels for 0%

profile of v2, /device:TPU:9, one launch (start us, length us, event | category | flops | bytes accessed | tf_op | source)
XLA Modules:
  0.0 175.7 jit_solution(5202656187428137019)
XLA Ops:
  0.7 1.4 reduce_sum.54
  2.1 1.4 multiply_reduce_fusion
  4.0 1.6 fusion
  7.7 3.1 %collective-permute-start = (bf16[256,384]{0,1:T(8,128)(2,1)}, bf16[256,384]{0,1:T(8,128)(2,1)}, u32[]{:S(2)}, u32[]{:S(2)}) collective-permute-start(bf16[256,384]{0,1:T(8,128)(2,1)} %bitcast.3), channel_id=1, source_target_pairs={{0,4},{4,8},{8,12},{12,16},{16,20},{20,24},{24,28},{1,5},{5,9},{9,... | collective-permute-start | bytes 589832 | tf_op jit(solution)/shard_map/ppermute | solution.py:21
  10.8 1.5 copy.55.input_weight_ref
  13.8 2.2 %broadcast_multiply_fusion = f32[256,768]{1,0:T(8,128)} fusion(f32[256,768]{1,0:T(8,128)} %param.29, f32[256]{0:T(256)S(1)} %get-tuple-element.92), kind=kLoop, calls=%fused_computation.26 | loop fusion | flops 196608 | bytes 1573888 | tf_op jit(solution)/shard_map/mul | solution.py:598
  16.0 1.6 copy.48
  17.6 1.6 copy.50
  19.3 1.6 constant_dynamic-slice_fusion.3.grad_y_ref
  21.1 1.7 copy.54.query_ref
  25.2 1.0 fusion.29
  26.1 1.6 fusion.34
  30.1 7.7 %shard_map.263 = f32[64,768]{1,0:T(8,128)S(1)} custom-call(bf16[4,64,768]{2,1,0:T(8,128)(2,1)S(1)} %bitcast.76), custom_call_target="tpu_custom_call" | custom-call | tf_op jit(solution)/shard_map/pallas_call | solution.py:79
  37.8 1.1 fusion.27
  40.4 6.7 %shard_map.264 = bf16[4,64,768]{2,1,0:T(8,128)(2,1)S(1)} custom-call(bf16[64,768]{1,0:T(8,128)(2,1)S(1)} %get-tuple-element.56.source), custom_call_target="tpu_custom_call" | custom-call | tf_op jit(solution)/shard_map/pallas_call | solution.py:120
  47.6 1.7 convolution_convert_fusion
  50.1 1.6 convolution_convert_fusion.1
  52.1 1.4 convolution_convert_fusion.3
  53.5 1.7 copy.53.attended_ref
  55.9 1.6 copy.47
  57.5 1.7 copy.49
  59.2 1.2 pad_maximum_fusion
  60.4 0.9 copy-done.2
  61.3 0.9 copy-done.3
  62.3 0.9 copy-done.4
  63.2 0.9 copy-done.5
  65.0 1.0 copy-done.7
  66.0 94.3 %shard_map.265 = (f32[64,768]{1,0:T(8,128)S(1)}, f32[64,768]{1,0:T(8,128)S(1)}, f32[96,576]{1,0:T(8,128)S(1)}, f32[96,192]{1,0:T(8,128)S(1)}, f32[96,768]{1,0:T(...) custom-call(bf16[4,64,768]{2,1,0:T(8,128)(2,1)S(1)} %bitcast.77, bf16[4,64,768]{2,1,0:T(8,128)(2,1)S(1)} %bitcast.75, ...), custom_call_target="tpu_custom_call" | custom-call | tf_op jit(solution)/shard_map/pallas_call | solution.py:439
  165.2 1.6 copy.57
  169.4 1.6 copy.66
  171.0 1.6 copy.67
  172.6 1.7 copy.68
  (116 shorter events, 22.7 us)
Async XLA Ops:
  0.6 48.7 %copy-start = (bf16[768,768]{1,0:T(8,128)(2,1)S(1)}, bf16[768,768]{1,0:T(8,128)(2,1)}, u32[]{:S(2)}) copy-start(bf16[768,768]{1,0:T(8,128)(2,1)} %param.27) | copy-start | bytes 3538948
  0.7 3.1 %copy-start.18 = (f32[256,768]{1,0:T(8,128)S(1)}, f32[256,768]{1,0:T(8,128)}, u32[]{:S(2)}) copy-start(f32[256,768]{1,0:T(8,128)} %param.16) | copy-start | bytes 2359300
  0.7 2.8 %copy-start.34 = (f32[384]{0:T(512)S(1)}, f32[384]{0:T(512)}, u32[]{:S(2)}) copy-start(f32[384]{0:T(512)} %param.20) | copy-start | bytes 4612
  0.7 3.1 %copy-start.26 = (f32[768]{0:T(1024)S(1)}, f32[768]{0:T(1024)}, u32[]{:S(2)}) copy-start(f32[768]{0:T(1024)} %param.17) | copy-start | bytes 9220
  0.7 3.1 %copy-start.28 = (f32[768]{0:T(1024)S(1)}, f32[768]{0:T(1024)}, u32[]{:S(2)}) copy-start(f32[768]{0:T(1024)} %param.18) | copy-start | bytes 9220
  5.6 2.1 %copy-start.25 = (bf16[256,576]{0,1:T(8,128)(2,1)}, bf16[256,576]{0,1:T(8,128)(2,1)S(1)}, u32[]{:S(2)}) copy-start(bf16[256,576]{0,1:T(8,128)(2,1)S(1)} %fusion) | copy-start | bytes 884740
  5.6 6.8 %copy-start.33 = (s32[8]{0:T(128)S(1)}, s32[8]{0:T(128)}, u32[]{:S(2)}) copy-start(s32[8]{0:T(128)} %param.31) | copy-start | bytes 100
  7.7 17.4 %collective-permute-start = (bf16[256,384]{0,1:T(8,128)(2,1)}, bf16[256,384]{0,1:T(8,128)(2,1)}, u32[]{:S(2)}, u32[]{:S(2)}) collective-permute-start(bf16[256,384]{0,1:T(8,128)(2,1)} %bitcast.3), channel_id=1, source_target_pairs={{0,4},{4,8},{8,12},{12,16},{16,20},{20,24},{24,28},{1,5},{5,9},{9,... | collective-permute-start | bytes 589832 | tf_op jit(solution)/shard_map/ppermute | solution.py:21
  12.4 10.4 %copy-start.27 = (f32[768]{0:T(1024)S(1)}, f32[768]{0:T(1024)}, u32[]{:S(2)}) copy-start(f32[768]{0:T(1024)} %param.23) | copy-start | bytes 9220
  12.4 10.3 %copy-start.32 = (f32[768]{0:T(1024)S(1)}, f32[768]{0:T(1024)}, u32[]{:S(2)}) copy-start(f32[768]{0:T(1024)} %param.28) | copy-start | bytes 9220
  26.1 2.1 %copy-start.24 = (bf16[256,3,64]{0,2,1:T(8,128)(2,1)}, bf16[256,3,64]{0,2,1:T(8,128)(2,1)S(1)}, u32[]{:S(2)}) copy-start(bf16[256,3,64]{0,2,1:T(8,128)(2,1)S(1)} %get-tuple-element.68) | copy-start | bytes 294916
  26.1 4.0 %copy-start.22 = (bf16[256,3,64]{0,2,1:T(8,128)(2,1)}, bf16[256,3,64]{0,2,1:T(8,128)(2,1)S(1)}, u32[]{:S(2)}) copy-start(bf16[256,3,64]{0,2,1:T(8,128)(2,1)S(1)} %get-tuple-element.67) | copy-start | bytes 294916
  28.6 1.5 copy-start.17
  28.6 1.2 copy-start.1
  28.6 9.2 %copy-start.29 = (f32[768]{0:T(1024)S(1)}, f32[768]{0:T(1024)}, u32[]{:S(2)}) copy-start(f32[768]{0:T(1024)} %param.22) | copy-start | bytes 9220
  28.6 11.0 %copy-start.30 = (f32[768]{0:T(1024)S(1)}, f32[768]{0:T(1024)}, u32[]{:S(2)}) copy-start(f32[768]{0:T(1024)} %param.24) | copy-start | bytes 9220
  29.0 1.1 copy-start.21
  29.8 17.3 %copy-start.19 = (bf16[768,768]{1,0:T(8,128)(2,1)S(1)}, bf16[768,768]{1,0:T(8,128)(2,1)}, u32[]{:S(2)}) copy-start(bf16[768,768]{1,0:T(8,128)(2,1)} %param.25) | copy-start | bytes 3538948
  29.8 17.3 %copy-start.31 = (f32[768]{0:T(1024)S(1)}, f32[768]{0:T(1024)}, u32[]{:S(2)}) copy-start(f32[768]{0:T(1024)} %param.26) | copy-start | bytes 9220
  39.6 8.0 %copy-start.20 = (f32[256,768]{1,0:T(8,128)S(1)}, f32[256,768]{1,0:T(8,128)}, u32[]{:S(2)}) copy-start(f32[256,768]{1,0:T(8,128)} %broadcast_multiply_fusion) | copy-start | bytes 2359300
  60.4 0.9 copy-start.2
  61.3 0.9 copy-start.3
  62.3 0.9 copy-start.4
  63.2 0.9 copy-start.5
  64.1 0.9 copy-start.6
  65.0 1.0 copy-start.7
  160.3 0.7 copy-start.8
  161.1 0.7 copy-start.10
  161.8 0.7 copy-start.12
  162.5 0.7 copy-start.13
  164.5 9.8 %copy-start.11 = (f32[96,768]{1,0:T(8,128)S(1)}, f32[96,768]{1,0:T(8,128)}, u32[]{:S(2)}) copy-start(f32[96,768]{1,0:T(8,128)} %copy-done.10) | copy-start | bytes 884740
  164.5 10.5 %copy-start.9 = (f32[96,768]{1,0:T(8,128)S(1)}, f32[96,768]{1,0:T(8,128)}, u32[]{:S(2)}) copy-start(f32[96,768]{1,0:T(8,128)} %copy-done.8) | copy-start | bytes 884740
  (4 other events, 2.5 us)

commit v3 on v2

--- a/solution.py
+++ b/solution.py
@@ -150,6 +150,41 @@
         jnp.sum(grad_in * normed, axis=0, keepdims=True),
         jnp.sum(grad_in, axis=0, keepdims=True),
     )
+
+
+def attention_kernel(heads, mixed_ref, prior_ref, allowed_ref, attended_ref, soft_ref):
+    b16 = jnp.bfloat16
+    for head in range(heads):
+        low = head * HEAD_DIM
+        first = 3 * low
+        second = first + HEAD_DIM
+        third = second + HEAD_DIM
+        keys = jnp.concatenate([prior_ref[:, second:third], mixed_ref[:, second:third]], axis=0)
+        values = jnp.concatenate(
+            [prior_ref[:, third : third + HEAD_DIM], mixed_ref[:, third : third + HEAD_DIM]], axis=0
+        )
+        scores = across(mixed_ref[:, first:second], keys, 1, 1) * HEAD_DIM ** (-0.5)
+        scores = jnp.where(allowed_ref[...] > 0.0, scores, -1e30)
+        row_top = jnp.max(scores, axis=-1, keepdims=True)
+        logsum = row_top + jnp.log(jnp.sum(jnp.exp(scores - row_top), axis=-1, keepdims=True))
+        soft = jnp.exp(scores - logsum)
+        soft_ref[head] = soft
+        attended_ref[:, low : low + HEAD_DIM] = across(soft.astype(b16), values, 1, 0).astype(b16)
+
+
+def attention(heads, mixed, prior, allowed):
+    vmem = pl.BlockSpec(memory_space=pltpu.VMEM)
+    rows = mixed.shape[0]
+    return pl.pallas_call(
+        functools.partial(attention_kernel, heads),
+        out_shape=[
+            jax.ShapeDtypeStruct((rows, heads * HEAD_DIM), jnp.bfloat16),
+            jax.ShapeDtypeStruct((heads, rows, 2 * rows), jnp.float32),
+        ],
+        in_specs=[vmem] * 3,
+        out_specs=[vmem] * 2,
+        compiler_params=pltpu.CompilerParams(vmem_limit_bytes=32 * 1024 * 1024),
+    )(mixed, prior, allowed)
 
 
 def tail_kernel(
@@ -170,9 +205,8 @@
     expand_bias_ref,
     attended_ref,
     output_weight_ref,
-    query_ref,
-    key_ref,
-    value_ref,
+    mixed_ref,
+    prior_ref,
     soft_ref,
     first_in_ref,
     input_weight_ref,
@@ -201,14 +235,26 @@
     mixed_grad,
     output_part,
     input_part,
+    reduce_mid,
+    expand_mid,
+    output_mid,
+    input_mid,
+    reduce_pair,
+    expand_pair,
+    output_pair,
+    input_pair,
+    reduce_land,
     expand_land,
-    reduce_land,
     output_land,
     input_land,
     tensor_send,
     tensor_recv,
-    dp_send,
-    dp_recv,
+    pair_send,
+    pair_recv,
+    line_send,
+    line_recv,
+    far_send,
+    far_recv,
     back_send,
     back_recv,
 ):
@@ -254,11 +300,67 @@
         return pltpu.make_async_remote_copy(
             src_ref=source(peer),
             dst_ref=target.at[step - 1],
-            send_sem=dp_send.at[kind, step - 1],
-            recv_sem=dp_recv.at[kind, step - 1],
+            send_sem=far_send.at[step - 1],
+            recv_sem=far_recv.at[step - 1],
             device_id={"dp": peer},
             device_id_type=mesh_id,
         )
+
+    half = shards // 2
+    parity = lax.rem(my_shard, 2)
+    place = my_shard // 2
+    partner = my_shard + 1 - 2 * parity
+
+    def pair_copy(kind, source, target, step):
+        return pltpu.make_async_remote_copy(
+            src_ref=source.at[2 * step + 1 - parity],
+            dst_ref=target.at[step],
+            send_sem=pair_send.at[kind, step],
+            recv_sem=pair_recv.at[kind, step],
+            device_id={"dp": partner},
+            device_id_type=mesh_id,
+        )
+
+    def line_copy(kind, source, target, step):
+        goal = lax.rem(place + step, half)
+        return pltpu.make_async_remote_copy(
+            src_ref=source.at[goal],
+            dst_ref=target.at[step - 1],
+            send_sem=line_send.at[kind, step - 1],
+            recv_sem=line_recv.at[kind, step - 1],
+            device_id={"dp": 2 * goal + parity},
+            device_id_type=mesh_id,
+        )
+
+    def begin_pair(kind, source, pair):
+        def run(step, carry):
+            pair_copy(kind, source, pair, step).start()
+            return carry
+
+        lax.fori_loop(0, half, run, 0)
+
+    def begin_line(kind, source, pair, mid, land):
+        def run(step, carry):
+            pair_copy(kind, source, pair, step).wait()
+            return carry
+
+        lax.fori_loop(0, half, run, 0)
+
+        def add(step, carry):
+            mid[step] = (
+                source[2 * step + parity].astype(f32) + pair[step].astype(f32)
+            ).astype(b16)
+            return carry
+
+        lax.fori_loop(0, half, add, 0)
+        begin(line_copy, kind, mid, land, half)
+
+    def end_line(kind, source, pair, mid, land, result):
+        finish(line_copy, kind, mid, land, half)
+        total = source[my_shard].astype(f32) + pair[place].astype(f32)
+        for step in range(half - 1):
+            total = total + land[step].astype(f32)
+        result[...] = total
 
     def begin(copy, kind, source, target, count):
         def run(step, carry):
@@ -279,11 +381,7 @@
     rows_move = (tensor_copy, 2, lambda p: rows16, lambda t: rows_all.at[my_group], groups)
     norm1_move = (tensor_copy, 3, lambda p: norm1_part.at[p], lambda t: norm1_land.at[t - 1], groups)
     vector_move = (tensor_copy, 4, lambda p: vector_part, lambda t: vector_land.at[t - 1], groups)
-    reduce_move = (dp_copy, 0, lambda p: reduce_ref.at[p], reduce_land, shards)
-    expand_move = (dp_copy, 1, lambda p: expand_ref.at[p], expand_land, shards)
-    output_move = (dp_copy, 2, lambda p: output_part.at[p], output_land, shards)
-    input_move = (dp_copy, 3, lambda p: input_part.at[p], input_land, shards)
-    far_move = (dp_copy, 4, lambda p: vector_own, vector_far, shards)
+    far_move = (dp_copy, 0, lambda p: vector_own.at[p], vector_far, shards)
 
     def total_of(own, land, count):
         total = own.astype(f32)
@@ -292,7 +390,7 @@
         return total
 
     begin(*norm2_move)
-    begin(*reduce_move)
+    begin_pair(0, reduce_ref, reduce_pair)
     begin(*feed_move)
     vector_part[...] = jnp.zeros_like(vector_part)
     finish(*norm2_move)
@@ -316,6 +414,7 @@
     feed_rows = total_of(feed_ref[my_group], feed_land, groups)
     block_out[...] = live_ref[...] * (hidden_ref[...] + feed_rows + reduce_bias_ref[...])
     finish(*rows_move)
+    begin_pair(1, expand_ref, expand_pair)
     share = rows_all.shape[1]
     rows = groups * share
     hidden16 = rows_all[...].reshape(rows, width)
@@ -327,12 +426,17 @@
         high = low + HEAD_DIM
         first = 3 * low
         att = grad_att[:, low:high]
-        keys = key_ref[:, low:high]
+        second = first + HEAD_DIM
+        third = second + HEAD_DIM
+        keys = jnp.concatenate([prior_ref[:, second:third], mixed_ref[:, second:third]], axis=0)
+        values = jnp.concatenate(
+            [prior_ref[:, third : third + HEAD_DIM], mixed_ref[:, third : third + HEAD_DIM]], axis=0
+        )
         soft = soft_ref[head]
-        grad_soft = across(att, value_ref[:, low:high], 1, 1)
+        grad_soft = across(att, values, 1, 1)
         delta = jnp.sum(soft * grad_soft, axis=-1, keepdims=True)
         grad_scores = (scale * soft * (grad_soft - delta)).astype(b16)
-        grad_keys = across(grad_scores, query_ref[:, low:high], 0, 0)
+        grad_keys = across(grad_scores, mixed_ref[:, first:second], 0, 0)
         grad_values = across(soft.astype(b16), att, 0, 0)
         back_own[:, low:high] = grad_keys[:rows].astype(b16)
         back_own[:, span + low : span + high] = grad_values[:rows].astype(b16)
@@ -353,12 +457,12 @@
     def _():
         back_copy.start()
 
-    begin(*expand_move)
+    begin_line(0, reduce_ref, reduce_pair, reduce_mid, reduce_land)
     output_grad = across(hidden16, attended_ref[...], 0, 0)
     piece = output_part.shape[1]
     for part in range(shards):
         output_part[part] = output_grad[part * piece : (part + 1) * piece].astype(b16)
-    begin(*output_move)
+    begin_pair(2, output_part, output_pair)
 
     @pl.when(my_shard < shards - 1)
     def _():
@@ -385,9 +489,18 @@
     input_grad = across(first_in_ref[...], mixed16, 0, 0)
     for part in range(shards):
         input_part[part] = input_grad[part * piece : (part + 1) * piece].astype(b16)
-    begin(*input_move)
-    vector_part[7:8, : mixed.shape[1]] = jnp.sum(mixed, axis=0, keepdims=True)
+    begin_pair(3, input_part, input_pair)
+    begin_line(1, expand_ref, expand_pair, expand_mid, expand_land)
+    bias_row = jnp.sum(mixed, axis=0, keepdims=True)
+    for head in range(heads):
+        first = 3 * head * HEAD_DIM
+        goes = 2 * head * HEAD_DIM
+        vector_part[7:8, goes : goes + HEAD_DIM] = bias_row[:, first : first + HEAD_DIM]
+        vector_part[7:8, goes + HEAD_DIM : goes + 2 * HEAD_DIM] = bias_row[
+            :, first + 2 * HEAD_DIM : first + 3 * HEAD_DIM
+        ]
     finish(*norm1_move)
+    begin_line(2, output_part, output_pair, output_mid, output_land)
     grad_norm1 = total_of(norm1_part[my_group], norm1_land, groups)
     back1, gain_row, shift_row = norm_back_rows(
         grad_norm1, normed1_ref[...], recip1_ref[...], gain1_ref[...]
@@ -402,23 +515,24 @@
     for step in range(1, groups - 1):
         added = added + vector_land[step]
     row_index = lax.broadcasted_iota(jnp.int32, own.shape, 0)
-    vector_own[...] = own + jnp.where(row_index < 6, added, 0.0)
+    own = own + jnp.where(row_index < 6, added, 0.0)
+    narrow = 2 * span // shards
+    for part in range(shards):
+        vector_own[part] = own[:, part * piece : (part + 1) * piece]
+        vector_own[part, 7:8, :narrow] = own[7:8, part * narrow : (part + 1) * narrow]
     begin(*far_move)
+    begin_line(3, input_part, input_pair, input_mid, input_land)
 
     @pl.when(my_shard > 0)
     def _():
         back_copy.wait_send()
 
-    finish(*reduce_move)
-    reduce_sum[...] = total_of(reduce_ref[my_shard], reduce_land, shards)
-    finish(*expand_move)
-    expand_sum[...] = total_of(expand_ref[my_shard], expand_land, shards)
-    finish(*output_move)
-    output_sum[...] = total_of(output_part[my_shard], output_land, shards)
-    finish(*input_move)
-    input_sum[...] = total_of(input_part[my_shard], input_land, shards)
+    end_line(0, reduce_ref, reduce_pair, reduce_mid, reduce_land, reduce_sum)
+    end_line(1, expand_ref, expand_pair, expand_mid, expand_land, expand_sum)
+    end_line(2, output_part, output_pair, output_mid, output_land, output_sum)
     finish(*far_move)
-    vector_sum[...] = total_of(vector_own[...], vector_far, shards)
+    vector_sum[...] = total_of(vector_own[my_shard], vector_far, shards)
+    end_line(3, input_part, input_pair, input_mid, input_land, input_sum)
 
 
 def tail(shards, groups, heads, operands):
@@ -430,6 +544,8 @@
     hidden = operands[2].shape[2]
     span = heads * HEAD_DIM
     broad = max(width, hidden, 3 * span)
+    half = shards // 2
+    sizes = (hidden, hidden, span, 3 * span)
     vmem = pl.BlockSpec(memory_space=pltpu.VMEM)
 
     def shape(*sizes):
@@ -445,7 +561,7 @@
             shape(piece, span),
             shape(piece, hidden),
             shape(piece, hidden),
-            shape(8, broad),
+            shape(8, piece),
         ],
         in_specs=[vmem] * len(operands),
         out_specs=[vmem] * 7,
@@ -458,21 +574,24 @@
             pltpu.VMEM((groups - 1, share, width), b16),
             pltpu.VMEM((8, broad), f32),
             pltpu.VMEM((groups - 1, 8, broad), f32),
-            pltpu.VMEM((8, broad), f32),
-            pltpu.VMEM((shards - 1, 8, broad), f32),
+            pltpu.VMEM((shards, 8, piece), f32),
+            pltpu.VMEM((shards - 1, 8, piece), f32),
             pltpu.VMEM((rows, 2 * span), b16),
             pltpu.VMEM((rows, 2 * span), b16),
             pltpu.VMEM((rows, 3 * span), f32),
             pltpu.VMEM((shards, piece, span), b16),
             pltpu.VMEM((shards, piece, 3 * span), b16),
-            pltpu.VMEM((shards - 1, piece, hidden), b16),
-            pltpu.VMEM((shards - 1, piece, hidden), b16),
-            pltpu.VMEM((shards - 1, piece, span), b16),
-            pltpu.VMEM((shards - 1, piece, 3 * span), b16),
+            *[pltpu.VMEM((half, piece, size), b16) for size in sizes],
+            *[pltpu.VMEM((half, piece, size), b16) for size in sizes],
+            *[pltpu.VMEM((half - 1, piece, size), b16) for size in sizes],
             dma((5, groups - 1)),
             dma((5, groups - 1)),
-            dma((5, shards - 1)),
-            dma((5, shards - 1)),
+            dma((4, half)),
+            dma((4, half)),
+            dma((4, half - 1)),
+            dma((4, half - 1)),
+            dma((shards - 1,)),
+            dma((shards - 1,)),
             dma,
             dma,
         ],
@@ -503,13 +622,6 @@
     return jnp.stack([shaped[:, 0], jnp.zeros_like(shaped[:, 0]), shaped[:, 1]], axis=1).reshape(
         group_heads * 3 * HEAD_DIM
     )
-
-
-def masked_scores(queries, key_rows, allowed):
-    scores = jnp.einsum(
-        "qhd,khd->hqk", queries, key_rows, preferred_element_type=jnp.float32
-    ) * HEAD_DIM ** (-0.5)
-    return jnp.where(allowed[None], scores, -1e30)
 
 
 def per_device(
@@ -535,7 +647,6 @@
     block_rows = block_input.shape[0]
     group_heads = output_weight.shape[0] // HEAD_DIM
     group_width = group_heads * HEAD_DIM
-    score_scale = HEAD_DIM ** (-0.5)
     tensor_count = lax.axis_size("tensor")
     share_rows = block_rows // tensor_count
     row_start = lax.axis_index("tensor") * share_rows
@@ -564,24 +675,9 @@
     mixed = jnp.dot(first_in, input_weight, preferred_element_type=f32) + full_bias(
         input_bias, group_heads
     )
-    mixed = mixed.astype(b16).reshape(block_rows, group_heads, 3, HEAD_DIM)
-    queries = mixed[:, :, 0]
-    own_pair = jnp.concatenate([mixed[:, :, 1], mixed[:, :, 2]], axis=1).reshape(
-        block_rows, 2 * group_width
-    )
-    prior_pair = from_behind(own_pair, "dp", 1).reshape(block_rows, 2 * group_heads, HEAD_DIM)
-    key_rows = jnp.concatenate([prior_pair[:, :group_heads], mixed[:, :, 1]], axis=0)
-    value_rows = jnp.concatenate([prior_pair[:, group_heads:], mixed[:, :, 2]], axis=0)
-    scores = masked_scores(queries, key_rows, allowed)
-    row_top = jnp.max(scores, axis=-1, keepdims=True)
-    logsum = row_top + jnp.log(jnp.sum(jnp.exp(scores - row_top), axis=-1, keepdims=True))
-    soft = jnp.exp(scores - logsum)
-    soft16 = soft.astype(b16)
-    attended = (
-        jnp.einsum("hqk,khd->qhd", soft16, value_rows, preferred_element_type=f32)
-        .astype(b16)
-        .reshape(block_rows, group_width)
-    )
+    mixed16 = mixed.astype(b16)
+    prior_mixed = from_behind(mixed16, "dp", 1)
+    attended, soft = attention(group_heads, mixed16, prior_mixed, allowed.astype(f32))
     in_shares = (tensor_count, share_rows, block_input.shape[1])
     (mixed_rows,) = scatter_sum(
         [jnp.dot(attended, output_weight, preferred_element_type=f32).astype(b16).reshape(in_shares)],
@@ -609,9 +705,6 @@
 
     def pieces(value):
         return value.reshape(shard_count, value.shape[0] // shard_count, value.shape[1])
-
-    def two_rows(values):
-        return values.reshape(values.shape[0], group_width)
 
     block_output, input_grad, input_sum, output_sum, expand_sum, reduce_sum, vectors = tail(
         shard_count,
@@ -632,9 +725,8 @@
             expand_bias_grad[None],
             attended,
             output_weight,
-            two_rows(queries),
-            two_rows(key_rows),
-            two_rows(value_rows),
+            mixed16,
+            prior_mixed,
             soft,
             first_in,
             input_weight,
@@ -643,32 +735,21 @@
             first_gain[None],
         ],
     )
-    features = block_input.shape[1]
-    bias_pairs = vectors[7, : 3 * group_width].reshape(group_heads, 3, HEAD_DIM)
-    input_bias_grad = jnp.stack([bias_pairs[:, 0], bias_pairs[:, 2]], axis=1).reshape(
-        2 * group_width
-    )
-
-    def own_piece(value):
-        size = value.shape[-1] // shard_count
-        return lax.dynamic_slice_in_dim(value, shard_index * size, size, value.ndim - 1)
-
-    vector_total = own_piece(vectors[:6, :features])
     return (
         block_output,
         input_grad,
-        vector_total[0],
-        vector_total[1],
+        vectors[0],
+        vectors[1],
         input_sum,
-        own_piece(input_bias_grad),
+        vectors[7, : input_bias.shape[0] // shard_count],
         output_sum.T,
-        vector_total[2],
-        vector_total[3],
-        vector_total[4],
+        vectors[2],
+        vectors[3],
+        vectors[4],
         expand_sum,
-        own_piece(vectors[6, : expand_bias_grad.shape[0]]),
+        vectors[6],
         reduce_sum.T,
-        vector_total[5],
+        vectors[5],
     )
 
 

time: 179 us -> 136 us (0.76); the launches traced: 176 us -> 135 us
  Pallas kernels: 109 us -> 85.5 us
  local copies, waits for them, and re-layouts: 40.6 us -> 28 us
  other arithmetic: 12 us -> 8.13 us
    pallas_call x1, Pallas kernels: 94.3 us -> 69.3 us  [tail(): pl.pallas_call(functools.partial(tail_kernel, shards, groups, heads), out...]
    concatenate x4 -> x0, local copies, waits for them, and re-layouts: 6.59 us -> none  [the longest x2 3.31 us: per_device(): jnp.concatenate([prior_pair[:, group_heads:], mixed[:, :, 2]], axis=0)]
    dynamic_slice x3 -> x0, local copies, waits for them, and re-layouts: 1.93 us -> none  [own_piece(): lax.dynamic_slice_in_dim(value, shard_index * size, size, value.ndim - 1)]
    dot_general x2 -> x0, matrix products: 1.92 us -> none  [the longest x1 1.55 us: masked_scores(): jnp.einsum('qhd,khd->hqk', queries, key_rows, preferred_element_type=jnp....]
    concatenate x3 -> x0, other arithmetic: 1.9 us -> none  [the longest x1 1.18 us: per_device(): jnp.concatenate([prior_pair[:, :group_heads], mixed[:, :, 1]], axis=0)]
    unnamed x77 -> x75, local copies, waits for them, and re-layouts: 21.2 us -> 21.3 us
  transfers between devices with their start and end apart: 1 -> 1, of which waited for: 0 -> 0; matrix products, arithmetic and copies ran while one was open for 8% -> 6% of each run, Pallas kernels for 0% -> 0%
where the time goes in v3:
time: 136 us; the launch traced here: 135 us
  Pallas kernels  85.5 us (63%)
  local copies, waits for them, and re-layouts  28 us (21%)
  matrix products  9.31 us (7%)
  other arithmetic  8.13 us (6%)
  starting transfers between devices  3.12 us (2%)
    pallas_call x1, Pallas kernels, tail(): pl.pallas_call(functools.partial(tail_kernel, shards, groups, heads), out...  69.3 us
    unnamed x75, local copies, waits for them, and re-layouts  21.3 us
    pallas_call x1, Pallas kernels, scatter_sum(): pl.pallas_call(functools.partial(scatter_kernel, axis, count, parts), out...  7.93 us
    pallas_call x1, Pallas kernels, gather(): pl.pallas_call(functools.partial(gather_kernel, axis, count), out_shape=j...  6.71 us
    ppermute x1, starting transfers between devices, from_behind(): lax.ppermute(value, axis, [(source, source + steps) for source in range(f...  3.12 us
  transfers between devices with their start and end apart: 1, of which 0 were waited for; matrix products, arithmetic and copies ran while one was open for 6% of the time, Pallas kernels for 0%

profile of v3, /device:TPU:9, one launch (start us, length us, event | category | flops | bytes accessed | tf_op | source)
XLA Modules:
  0.0 135.2 jit_solution(4530290541465484710)
XLA Ops:
  0.7 1.4 %reduce_sum.45 = f32[256]{0:T(256)S(1)} reduce(f32[256,768]{1,0:T(8,128)} %param.16, f32[]{:T(128)} %constant.10.clone.1), dimensions={1}, to_apply=%region_0.0 | reduce | flops 196352 | bytes 787460 | tf_op jit(solution)/shard_map/reduce_sum | solution.py:605
  2.7 1.1 add_convert_fusion
  3.8 1.7 %fusion.mixed_ref = bf16[256,576]{1,0:T(8,128)(2,1)S(1)} fusion(bf16[256,768]{1,0:T(8,128)(2,1)S(1)} %get-tuple-element.50.first_in_ref, bf16[768,576]{0,1:T(8,128)(2,1)} %param.19, f32[576]{0:T(1024)S(1)} %add.113), kind=kOutput, calls=%fused_computation.8 | convolution fusion | flops 226787328 | bytes 1575168 | tf_op jit(solution)/shard_map/dot_general | solution.py:675
  5.5 3.1 %collective-permute-start = (bf16[256,576]{1,0:T(8,128)(2,1)S(1)}, bf16[256,576]{1,0:T(8,128)(2,1)S(1)}, u32[]{:S(2)}, u32[]{:S(2)}) collective-permute-start(bf16[256,576]{1,0:T(8,128)(2,1)S(1)} %fusion.mixed_ref), channel_id=1, source_target_pairs={{0,4},{4,8},{8,12},{12,16},{16,20},{20,24},{24,28},{1,5},{5,9},{9,... | collective-permute-start | bytes 884744 | tf_op jit(solution)/shard_map/ppermute | solution.py:21
  10.0 1.3 broadcast_multiply_fusion
  12.6 0.8 fusion.16
  13.7 1.5 %copy.33.input_weight_ref = bf16[768,576]{1,0:T(8,128)(2,1)S(1)} copy(bf16[768,576]{0,1:T(8,128)(2,1)} %param.19) | data formatting | bytes 1769472 | tf_op args[3]
  15.5 1.6 %constant_dynamic-slice_fusion.normed1_ref = f32[64,768]{1,0:T(8,128)} fusion(f32[256,768]{1,0:T(8,128)} %get-tuple-element.51, s32[]{:T(128)S(6)} %select_n.8), kind=kLoop, calls=%fused_computation.40 | loop fusion | bytes 393220 | tf_op jit(solution)/shard_map/dynamic_slice | solution.py:655
  17.2 1.6 %shard_map.263 = (bf16[256,192]{1,0:T(8,128)(2,1)S(1)}, f32[3,256,512]{2,1,0:T(8,128)S(1)}) custom-call(bf16[256,576]{1,0:T(8,128)(2,1)S(1)} %fusion.mixed_ref, bf16[256,576]{1,0:T(8,128)(2,1)S(1)} %collective-permute-done.prior_ref, f32[256,512]{1,0:T(8,128)S(1)} %add_convert_fusion.1.allowed_ref), custom_call_target="tpu_custom_call" | custom-call | tf_op jit(solution)/shard_map/pallas_call | solution.py:178
  18.8 1.2 copy-done.1
  20.0 1.3 convolution_convert_fusion.4
  21.3 7.9 %shard_map.264 = f32[64,768]{1,0:T(8,128)S(1)} custom-call(bf16[4,64,768]{2,1,0:T(8,128)(2,1)S(1)} %bitcast.48), custom_call_target="tpu_custom_call" | custom-call | tf_op jit(solution)/shard_map/pallas_call | solution.py:79
  29.3 1.1 fusion.15
  31.1 0.8 add_convert_fusion.2
  31.8 6.7 %shard_map.265 = bf16[4,64,768]{2,1,0:T(8,128)(2,1)S(1)} custom-call(bf16[64,768]{1,0:T(8,128)(2,1)S(1)} %get-tuple-element.46.source), custom_call_target="tpu_custom_call" | custom-call | tf_op jit(solution)/shard_map/pallas_call | solution.py:120
  39.1 1.4 %convolution_convert_fusion.3 = bf16[256,768]{1,0:T(8,128)(2,1)} fusion(bf16[768,768]{1,0:T(8,128)(2,1)S(1)} %copy-done, f32[256,768]{1,0:T(8,128)S(1)} %convolution_add_fusion), kind=kOutput, calls=%fused_computation.6 | convolution fusion | flops 303955968 | bytes 2359296 | tf_op jit(solution)/shard_map/dot_general | solution.py:693
  40.5 0.8 fusion.19
  41.2 1.7 %convolution_convert_fusion = bf16[768,768]{1,0:T(8,128)(2,1)} fusion(f32[256,768]{1,0:T(8,128)S(1)} %copy-done.24, f32[256,768]{1,0:T(8,128)S(1)} %convolution_add_fusion), kind=kOutput, calls=%fused_computation | convolution fusion | flops 304545792 | bytes 2752512 | tf_op jit(solution)/shard_map/rd,rk->dk/dot_general | solution.py:704
  43.4 1.5 %convolution_convert_fusion.1 = bf16[768,768]{1,0:T(8,128)(2,1)} fusion(bf16[256,768]{1,0:T(8,128)(2,1)S(1)} %bitcast.46, bf16[256,768]{1,0:T(8,128)(2,1)S(1)} %get-tuple-element.70), kind=kOutput, calls=%fused_computation.1 | convolution fusion | flops 302579712 | bytes 1966080 | tf_op jit(solution)/shard_map/rd,rk->dk/dot_general | solution.py:703
  45.0 1.4 %copy.31.recip2_ref = f32[64,1]{1,0:T(8,128)} copy(f32[64,1]{0,1:T(1,128)} %get-tuple-element.65) | data formatting | bytes 512 | tf_op jit(solution)/shard_map/rsqrt | solution.py:606
  46.3 1.0 copy-done.3
  47.3 1.0 copy-done.4
  48.3 0.9 copy-done.5
  49.2 0.9 copy-done.6
  50.1 0.9 copy-done.7
  51.1 0.9 copy-done.9
  52.0 1.0 copy-done.10
  53.0 0.8 copy-done.19
  53.7 69.3 %shard_map.266 = (f32[64,768]{1,0:T(8,128)S(1)}, f32[64,768]{1,0:T(8,128)S(1)}, f32[96,576]{1,0:T(8,128)S(1)}, f32[96,192]{1,0:T(8,128)S(1)}, f32[96,768]{1,0:T(...) custom-call(bf16[4,64,768]{2,1,0:T(8,128)(2,1)S(1)} %bitcast.49, bf16[4,64,768]{2,1,0:T(8,128)(2,1)S(1)} %bitcast.47, ...), custom_call_target="tpu_custom_call" | custom-call | tf_op jit(solution)/shard_map/pallas_call | solution.py:555
  128.2 1.6 %copy.35 = f32[192,96]{1,0:T(8,128)} copy(f32[192,96]{0,1:T(8,128)} %bitcast.51) | data formatting | bytes 147456
  129.8 1.6 %copy.42 = f32[64,768]{1,0:T(8,128)} copy(f32[64,768]{1,0:T(8,128)} %copy-done.18) | data formatting | bytes 393216
  131.4 1.6 %copy.43 = f32[64,768]{1,0:T(8,128)} copy(f32[64,768]{1,0:T(8,128)} %copy-done.17) | data formatting | bytes 393216
  (92 shorter events, 12.8 us)
Async XLA Ops:
  0.6 38.4 %copy-start = (bf16[768,768]{1,0:T(8,128)(2,1)S(1)}, bf16[768,768]{1,0:T(8,128)(2,1)}, u32[]{:S(2)}) copy-start(bf16[768,768]{1,0:T(8,128)(2,1)} %param.27) | copy-start | bytes 3538948
  0.7 1.5 %copy-start.21 = (f32[256,768]{1,0:T(8,128)S(1)}, f32[256,768]{1,0:T(8,128)}, u32[]{:S(2)}) copy-start(f32[256,768]{1,0:T(8,128)} %param.16) | copy-start | bytes 2359300
  0.7 1.7 %copy-start.33 = (f32[384]{0:T(512)S(1)}, f32[384]{0:T(512)}, u32[]{:S(2)}) copy-start(f32[384]{0:T(512)} %param.20) | copy-start | bytes 4612
  0.7 2.0 %copy-start.25 = (f32[768]{0:T(1024)S(1)}, f32[768]{0:T(1024)}, u32[]{:S(2)}) copy-start(f32[768]{0:T(1024)} %param.17) | copy-start | bytes 9220
  0.7 2.0 %copy-start.27 = (f32[768]{0:T(1024)S(1)}, f32[768]{0:T(1024)}, u32[]{:S(2)}) copy-start(f32[768]{0:T(1024)} %param.18) | copy-start | bytes 9220
  3.8 4.9 %copy-start.32 = (s32[8]{0:T(128)S(1)}, s32[8]{0:T(128)}, u32[]{:S(2)}) copy-start(s32[8]{0:T(128)} %param.31) | copy-start | bytes 100
  5.5 11.7 %collective-permute-start = (bf16[256,576]{1,0:T(8,128)(2,1)S(1)}, bf16[256,576]{1,0:T(8,128)(2,1)S(1)}, u32[]{:S(2)}, u32[]{:S(2)}) collective-permute-start(bf16[256,576]{1,0:T(8,128)(2,1)S(1)} %fusion.mixed_ref), channel_id=1, source_target_pairs={{0,4},{4,8},{8,12},{12,16},{16,20},{20,24},{24,28},{1,5},{5,9},{9,... | collective-permute-start | bytes 884744 | tf_op jit(solution)/shard_map/ppermute | solution.py:21
  11.2 2.5 %copy-start.23 = (f32[256,768]{1,0:T(8,128)}, f32[256,768]{1,0:T(8,128)S(1)}, u32[]{:S(2)}) copy-start(f32[256,768]{1,0:T(8,128)S(1)} %broadcast_multiply_fusion) | copy-start | bytes 2359300
  11.2 4.0 %copy-start.31 = (f32[768]{0:T(1024)S(1)}, f32[768]{0:T(1024)}, u32[]{:S(2)}) copy-start(f32[768]{0:T(1024)} %param.28) | copy-start | bytes 9220
  11.3 4.0 %copy-start.26 = (f32[768]{0:T(1024)S(1)}, f32[768]{0:T(1024)}, u32[]{:S(2)}) copy-start(f32[768]{0:T(1024)} %param.23) | copy-start | bytes 9220
  17.2 12.1 %copy-start.28 = (f32[768]{0:T(1024)S(1)}, f32[768]{0:T(1024)}, u32[]{:S(2)}) copy-start(f32[768]{0:T(1024)} %param.22) | copy-start | bytes 9220
  17.2 12.1 %copy-start.2 = (bf16[256,576]{1,0:T(8,128)(2,1)}, bf16[256,576]{1,0:T(8,128)(2,1)S(1)}, u32[]{:S(2)}) copy-start(bf16[256,576]{1,0:T(8,128)(2,1)S(1)} %collective-permute-done.prior_ref) | copy-start | bytes 884740
  18.8 1.2 copy-start.1
  20.0 1.3 copy-start.8
  20.0 11.1 %copy-start.29 = (f32[768]{0:T(1024)S(1)}, f32[768]{0:T(1024)}, u32[]{:S(2)}) copy-start(f32[768]{0:T(1024)} %param.24) | copy-start | bytes 9220
  21.3 17.3 %copy-start.22 = (bf16[768,768]{1,0:T(8,128)(2,1)S(1)}, bf16[768,768]{1,0:T(8,128)(2,1)}, u32[]{:S(2)}) copy-start(bf16[768,768]{1,0:T(8,128)(2,1)} %param.25) | copy-start | bytes 3538948
  21.3 17.3 %copy-start.30 = (f32[768]{0:T(1024)S(1)}, f32[768]{0:T(1024)}, u32[]{:S(2)}) copy-start(f32[768]{0:T(1024)} %param.26) | copy-start | bytes 9220
  39.1 1.4 %copy-start.24 = (f32[256,768]{1,0:T(8,128)S(1)}, f32[256,768]{1,0:T(8,128)}, u32[]{:S(2)}) copy-start(f32[256,768]{1,0:T(8,128)} %copy-done.23) | copy-start | bytes 2359300
  46.3 1.0 copy-start.3
  47.3 1.0 copy-start.4
  48.3 0.9 copy-start.5
  49.2 0.9 copy-start.6
  50.1 0.9 copy-start.7
  51.1 0.9 copy-start.9
  52.0 1.0 copy-start.10
  53.0 0.8 copy-start.19
  123.0 0.7 copy-start.11
  123.7 0.7 copy-start.13
  124.4 0.7 copy-start.15
  127.1 5.9 %copy-start.16 = (f32[96,576]{1,0:T(8,128)S(1)}, f32[96,576]{1,0:T(8,128)}, u32[]{:S(2)}) copy-start(f32[96,576]{1,0:T(8,128)} %copy-done.15) | copy-start | bytes 663556
  127.1 6.6 %copy-start.14 = (f32[96,768]{1,0:T(8,128)S(1)}, f32[96,768]{1,0:T(8,128)}, u32[]{:S(2)}) copy-start(f32[96,768]{1,0:T(8,128)} %copy-done.13) | copy-start | bytes 884740
  127.1 7.3 %copy-start.12 = (f32[96,768]{1,0:T(8,128)S(1)}, f32[96,768]{1,0:T(8,128)}, u32[]{:S(2)}) copy-start(f32[96,768]{1,0:T(8,128)} %copy-done.11) | copy-start | bytes 884740
  (3 other events, 2.0 us)
